TPU v7x, 256 devices: a whole 4x4x8 slice. The times are simulated.
256 devices in a mesh: flow: 16 (over z, x_hi), grad: 16 (over y, x_lo, core).
Axes of the slice: x: 4 (x_hi: 2, x_lo: 2; x = x_hi * 2 + x_lo), y: 4, z: 8, core: 2. Of those that a mesh axis runs over, the one named last changes fastest.
Arguments:
- populations: float32 [19, 128, 128, 128], P(None, 'flow', 'grad'), may hold values from 0.008 to 1.01, as said below
- le_offset: int32 [1], replicated, may hold values from 0 to 127
- sphere_velocity: float32 [3, 16, 16, 64], P(None, 'flow', 'grad'), may hold values from -0.4 to 0.4
- link_cell: int32 [16, 16, 16384], P('flow', 'grad'), may hold values from 0 to 8191, as said below
- link_dir: int32 [16, 16, 16384], P('flow', 'grad'), may hold values from 1 to 18, as said below
- link_sphere: int32 [16, 16, 16384], P('flow', 'grad'), may hold values from 0 to 575
- link_count: int32 [16, 16], P('flow', 'grad'), may hold values from 4096 to 16384, as said below
- pair_first: int32 [16, 16, 256], P('flow', 'grad'), may hold values from 0 to 63
- pair_second: int32 [16, 16, 256], P('flow', 'grad'), may hold values from 0 to 575
- pair_count: int32 [16, 16], P('flow', 'grad'), may hold values from 64 to 256, as said below
- pair_gap: float32 [16, 16, 256], P('flow', 'grad'), may hold values from 0.02 to 1
- pair_normal: float32 [3, 16, 16, 256], P(None, 'flow', 'grad'), may hold values from -1 to 1
Outputs:
- populations_next: float32 [19, 128, 128, 128], P(None, 'flow', 'grad')
- sphere_force: float32 [3, 16, 16, 64], P(None, 'flow', 'grad')
- velocity_next: float32 [3, 16, 16, 64], P(None, 'flow', 'grad')
Inputs may be any that keep to these rules, and one draw needn't show every extreme that they name: `populations`: each population lies between 0.3 and 3 times its direction's lattice weight. `link_cell`: local cell numbers (x_local * 8 + y_local) * 128 + z; within one tile no two link slots name the same cell and direction, and a cell may carry several links. `link_dir`: within one tile no two link slots name the same cell and direction. Live links of a tile are its first link_count slots; in every draw some tile has all 16384 slots live. Live pairs of a tile are its first pair_count slots; in every draw some tile has all 256 slots live.
All inputs are finite; a program needn't handle non-finite values.
Results may differ from a plain program's by a relative error of at most 0.0003.
Values sent between devices are 32-bit elements; how exact they have to be, the bound alone decides.
A program may use at most 64 MiB of HBM per device.

v0:
```python
import jax
import jax.numpy as jnp
from jax import lax
from jax.sharding import PartitionSpec as P

VELOCITIES = [
    (0, 0, 0),
    (1, 0, 0),
    (-1, 0, 0),
    (0, 1, 0),
    (0, -1, 0),
    (0, 0, 1),
    (0, 0, -1),
    (1, 1, 0),
    (-1, -1, 0),
    (1, -1, 0),
    (-1, 1, 0),
    (1, 0, 1),
    (-1, 0, -1),
    (1, 0, -1),
    (-1, 0, 1),
    (0, 1, 1),
    (0, -1, -1),
    (0, 1, -1),
    (0, -1, 1),
]
WEIGHTS = [1.0 / 3.0] + [1.0 / 18.0] * 6 + [1.0 / 36.0] * 12
XY_MOVING = [1, 2, 3, 4, 7, 8, 9, 10, 11, 12, 13, 14, 15, 16, 17, 18]
UPWARD = [3, 7, 10, 15, 17]
DOWNWARD = [4, 8, 9, 16, 18]
RELAX_TIME = 0.8
SHEAR_SPEED = 0.1
LUB_COEF = 0.5
GAP_FLOOR = 0.1
GAP_CUTOFF = 1.0
INV_MASS = 1.0 / 523.6


def from_behind(block, axis, distance):
    devices = range(lax.axis_size(axis))
    route = [((i - distance) % len(devices), i) for i in devices]
    return lax.ppermute(block, axis, route)


def padded(block, sides, width):
    for axis, dim in sides:
        count = lax.axis_size(axis)
        forward = [(i, i + 1) for i in range(count - 1)]
        forward.append((count - 1, 0))
        backward = [(target, source) for source, target in forward]
        low = lax.ppermute(
            lax.slice_in_dim(block, block.shape[dim] - width, None, axis=dim), axis, forward
        )
        high = lax.ppermute(lax.slice_in_dim(block, 0, width, axis=dim), axis, backward)
        block = jnp.concatenate([low, block, high], axis=dim)
    return block


def collide(populations):
    density = jnp.sum(populations, axis=0)
    speeds = []
    for axis_id in range(3):
        running = None
        for direction, vector in enumerate(VELOCITIES):
            if vector[axis_id] != 0:
                addend = vector[axis_id] * populations[direction]
                running = addend if running is None else running + addend
        speeds.append(running / density)
    speed_sq = speeds[0] * speeds[0] + speeds[1] * speeds[1] + speeds[2] * speeds[2]
    relaxed = []
    for direction, vector in enumerate(VELOCITIES):
        c_dot = None
        for axis_id in range(3):
            if vector[axis_id] != 0:
                addend = vector[axis_id] * speeds[axis_id]
                c_dot = addend if c_dot is None else c_dot + addend
        if c_dot is None:
            equil = WEIGHTS[direction] * density * (1.0 - 1.5 * speed_sq)
        else:
            equil = (
                WEIGHTS[direction]
                * density
                * (1.0 + 3.0 * c_dot + 4.5 * c_dot * c_dot - 1.5 * speed_sq)
            )
        current = populations[direction]
        relaxed.append(current - (current - equil) / RELAX_TIME)
    return (relaxed, density)


def tile_links(
    relaxed,
    density,
    propagated,
    near_speed,
    link_cell,
    link_dir,
    link_sphere,
    link_count,
    pair_first,
    pair_second,
    pair_count,
    pair_gap,
    pair_normal,
):
    n_cells = relaxed.shape[1]
    slot_count = near_speed.shape[1] // 9
    onehot = (link_dir[None, :] == lax.iota(jnp.int32, 19)[:, None]).astype(relaxed.dtype)
    lookup = jnp.asarray(
        [[vector[k] for vector in VELOCITIES] for k in range(3)] + [WEIGHTS], relaxed.dtype
    )
    picked = jnp.dot(lookup, onehot, precision=lax.Precision.HIGHEST)
    leaving = jnp.sum(onehot * relaxed[:, link_cell], axis=0)
    wall_speed = near_speed[:, link_sphere]
    c_dot_u = jnp.sum(picked[:3] * wall_speed, axis=0)
    bounced = leaving - 6.0 * picked[3] * density[link_cell] * c_dot_u
    is_live = lax.iota(jnp.int32, link_dir.shape[0]) < link_count
    opposite = jnp.where(link_dir % 2 == 1, link_dir + 1, link_dir - 1)
    target = jnp.where(is_live, opposite * n_cells + link_cell, 19 * n_cells)
    updated = propagated.reshape(-1).at[target].set(bounced, mode="drop").reshape(19, n_cells)
    link_force = picked[:3] * (leaving + bounced) * is_live.astype(relaxed.dtype)
    pair_live = (lax.iota(jnp.int32, pair_first.shape[0]) < pair_count).astype(relaxed.dtype)
    first_ref = pair_first + 4 * slot_count
    first_speed = near_speed[:, first_ref]
    second_speed = near_speed[:, pair_second]
    normal_rate = jnp.sum((first_speed - second_speed) * pair_normal, axis=0)
    resist = LUB_COEF * (1.0 / jnp.maximum(pair_gap, GAP_FLOOR) - 1.0 / GAP_CUTOFF)
    lubrication = -resist * normal_rate * pair_normal * pair_live
    sphere_refs = jnp.concatenate([link_sphere, first_ref, pair_second])
    values = jnp.concatenate([link_force, lubrication, -lubrication], axis=1)
    partial_value = jax.ops.segment_sum(values.T, sphere_refs, num_segments=9 * slot_count).T
    return (updated, partial_value)


def edge_slice(behind, ahead, cell_rest):
    width_x = ahead.shape[1]
    joined = jnp.concatenate([behind, ahead], axis=1)
    return lax.dynamic_slice_in_dim(joined, width_x - cell_rest, width_x, 1)


def rows_of(directions):
    return [XY_MOVING.index(direction) for direction in directions]


def boosts_of(directions):
    return jnp.asarray(
        [6.0 * WEIGHTS[d] * VELOCITIES[d][0] * SHEAR_SPEED for d in directions], jnp.float32
    )[:, None, None]


def per_device(
    populations,
    le_offset,
    sphere_velocity,
    link_cell,
    link_dir,
    link_sphere,
    link_count,
    pair_first,
    pair_second,
    pair_count,
    pair_gap,
    pair_normal,
):
    relaxed, density = collide(populations)
    width_x = populations.shape[1]
    width_y = populations.shape[2]
    depth = populations.shape[3]
    moving = jnp.stack([relaxed[direction] for direction in XY_MOVING])
    up_rows = rows_of(UPWARD)
    down_rows = rows_of(DOWNWARD)
    top_layer = moving[jnp.asarray(up_rows)][:, :, width_y - 1, :]
    bottom_layer = moving[jnp.asarray(down_rows)][:, :, 0, :]
    offset_cells = le_offset[0]
    flow_count = lax.axis_size("flow")
    span_x = flow_count * width_x
    amounts = jnp.stack([(span_x - offset_cells) % span_x, offset_cells])
    device_hops = amounts // width_x
    cell_rest = amounts % width_x
    hop_counts = jnp.concatenate([device_hops, (device_hops + 1) % flow_count])
    layers_now = jnp.stack([top_layer, bottom_layer, top_layer, bottom_layer])
    for level in range(max(flow_count - 1, 1).bit_length()):
        arrived = from_behind(layers_now, "flow", 1 << level)
        selected = hop_counts // (1 << level) % 2 == 1
        layers_now = jnp.where(selected[:, None, None, None], arrived, layers_now)
    top_moved = edge_slice(layers_now[2], layers_now[0], cell_rest[0])
    bottom_moved = edge_slice(layers_now[3], layers_now[1], cell_rest[1])
    grad_index = lax.axis_index("grad")
    grad_count = lax.axis_size("grad")
    top_send = jnp.where(grad_index == grad_count - 1, top_moved - boosts_of(UPWARD), top_layer)
    bottom_send = jnp.where(grad_index == 0, bottom_moved + boosts_of(DOWNWARD), bottom_layer)
    top_full = moving[:, :, width_y - 1, :].at[jnp.asarray(up_rows)].set(top_send)
    bottom_full = moving[:, :, 0, :].at[jnp.asarray(down_rows)].set(bottom_send)
    framed = jnp.concatenate([bottom_full[:, :, None], moving, top_full[:, :, None]], axis=2)
    rimmed = padded(framed, (("flow", 1), ("grad", 2)), 1)
    ghosted = jnp.concatenate(
        [rimmed[:, :, 0:1], rimmed[:, :, 2 : width_y + 2], rimmed[:, :, width_y + 3 :]], axis=2
    )
    propagated = []
    for direction, vector in enumerate(VELOCITIES):
        if direction in XY_MOVING:
            source = ghosted[
                XY_MOVING.index(direction),
                1 - vector[0] : 1 - vector[0] + width_x,
                1 - vector[1] : 1 - vector[1] + width_y,
                :,
            ]
        else:
            source = relaxed[direction]
        propagated.append(jnp.roll(source, vector[2], axis=2))
    slot_count = sphere_velocity.shape[3]
    rim_speed = padded(sphere_velocity, (("flow", 1), ("grad", 2)), 1)
    near_speed = rim_speed.reshape(3, 9 * slot_count)
    n_cells = width_x * width_y * depth
    updated, partial_value = tile_links(
        jnp.stack(relaxed).reshape(19, n_cells),
        density.reshape(n_cells),
        jnp.stack(propagated).reshape(19, n_cells),
        near_speed,
        link_cell[0, 0],
        link_dir[0, 0],
        link_sphere[0, 0],
        link_count[0, 0],
        pair_first[0, 0],
        pair_second[0, 0],
        pair_count[0, 0],
        pair_gap[0, 0],
        pair_normal[:, 0, 0],
    )
    gathered_parts = padded(
        partial_value.reshape(3, 1, 1, 9, slot_count), (("flow", 1), ("grad", 2)), 1
    )
    gathered_parts = jnp.flip(gathered_parts.reshape(3, 9, 9, slot_count), axis=2)
    own_force = jnp.sum(jnp.diagonal(gathered_parts, axis1=1, axis2=2), axis=-1)
    sphere_force = own_force[:, None, None, :]
    velocity_next = sphere_velocity + INV_MASS * sphere_force
    return (updated.reshape(19, width_x, width_y, depth), sphere_force, velocity_next)


def solution(mesh):
    in_specs = (
        P(None, "flow", "grad", None),
        P(),
        P(None, "flow", "grad", None),
        P("flow", "grad", None),
        P("flow", "grad", None),
        P("flow", "grad", None),
        P("flow", "grad"),
        P("flow", "grad", None),
        P("flow", "grad", None),
        P("flow", "grad"),
        P("flow", "grad", None),
        P(None, "flow", "grad", None),
    )
    out_specs = (
        P(None, "flow", "grad", None),
        P(None, "flow", "grad", None),
        P(None, "flow", "grad", None),
    )
    return jax.shard_map(
        per_device, mesh=mesh, in_specs=in_specs, out_specs=out_specs, check_vma=False
    )
```

profile of v0, /device:TPU:1, one launch (start us, length us, event | category | flops | bytes accessed | tf_op | source)
XLA Modules:
  0.0 467.0 jit_solution(11105814869026919376)
XLA Ops:
  0.7 3.7 collective-permute-start.8
  4.3 5.4 %collective-permute-start.9 = (f32[3,1,1,64]{3,2,1,0:T(1,128)}, f32[3,1,1,64]{3,2,1,0:T(1,128)S(1)}, u32[]{:S(2)}, u32[]{:S(2)}) collective-permute-start(f32[3,1,1,64]{3,2,1,0:T(1,128)} %param.21), channel_id=1, source_target_pairs={{16,0},{32,16},{48,32},{64,48},{80,64},{96,80},{112,96},{128,112},... | collective-permute-start | bytes 2312 | tf_op jit(solution)/shard_map/ppermute | solution.py:54
  9.7 1.1 reduce_sum.51
  10.8 1.1 multiply_subtract_fusion.1
  11.9 0.8 constant_dynamic-update-slice_fusion.15
  12.7 0.8 constant_dynamic-update-slice_fusion.14
  13.5 0.8 constant_dynamic-update-slice_fusion.13
  14.3 0.8 constant_dynamic-update-slice_fusion.12
  15.1 0.8 constant_dynamic-update-slice_fusion.11
  15.9 0.8 constant_dynamic-update-slice_fusion.10
  16.7 0.8 constant_dynamic-update-slice_fusion.9
  17.4 0.8 constant_dynamic-update-slice_fusion.8
  18.2 0.8 constant_dynamic-update-slice_fusion.7
  19.0 0.8 constant_dynamic-update-slice_fusion.6
  19.8 0.8 constant_dynamic-update-slice_fusion.5
  20.6 0.8 constant_dynamic-update-slice_fusion.4
  21.4 0.8 constant_dynamic-update-slice_fusion.3
  22.2 0.8 constant_dynamic-update-slice_fusion.2
  23.0 0.8 constant_dynamic-update-slice_fusion.1
  23.8 0.8 constant_dynamic-update-slice_fusion
  28.8 0.9 stack.164
  29.7 2.7 copy.185
  33.0 56.6 %gather_fusion.2 = f32[16384,19]{1,0:T(8,128)} fusion(f32[19,8192]{0,1:T(8,128)} %copy.185, s32[16384]{0:T(1024)S(1)} %get-tuple-element.99), kind=kCustom, calls=%fused_computation.2 | custom fusion | bytes 2555904 | tf_op jit(solution)/shard_map/gather | solution.py:112
  89.6 8.4 %fusion = f32[16384]{0:T(1024)S(1)} fusion(f32[16384,19]{1,0:T(8,128)} %gather_fusion.2, s32[16384]{0:T(1024)S(1)} %bitcast.441), kind=kLoop, calls=%fused_computation.13 | loop fusion | flops 917504 | bytes 1376256 | tf_op jit(solution)/shard_map/reduce_sum | solution.py:112
  98.0 5.8 %fusion.1 = f32[4,16384]{1,0:T(4,128)S(1)} fusion(f32[4,19]{1,0:T(4,128)S(1)} %copy-done.14, s32[16384]{0:T(1024)S(1)} %bitcast.442), kind=kOutput, calls=%fused_computation.15 | convolution fusion | flops 15253504 | bytes 327984 | tf_op jit(solution)/shard_map/dot_general | solution.py:111
  104.8 1.0 collective-permute-start.11
  105.9 0.8 collective-permute-start.10
  109.5 90.5 %gather_fusion.3 = f32[16384]{0:T(1024)S(1)} fusion(f32[8192]{0:T(1024)S(1)} %bitcast.398, s32[16384]{0:T(1024)S(1)} %get-tuple-element.99), kind=kCustom, calls=%fused_computation.3 | custom fusion | bytes 196608 | tf_op jit(solution)/shard_map/gather | solution.py:115
  200.3 54.4 %gather_fusion.4 = f32[16384,3]{1,0:T(8,128)} fusion(f32[3,576]{0,1:T(8,128)S(1)} %bitcast.401, s32[16384]{0:T(1024)S(1)} %get-tuple-element.98), kind=kCustom, calls=%fused_computation.4 | custom fusion | bytes 458752 | tf_op jit(solution)/shard_map/gather | solution.py:113
  254.7 5.4 %copy.187 = f32[16384,3]{0,1:T(4,128)S(1)} copy(f32[16384,3]{1,0:T(8,128)} %gather_fusion.4) | data formatting | bytes 393216 | tf_op jit(solution)/shard_map/gather | solution.py:113
  261.0 0.7 gather_fusion.6
  262.4 4.9 %copy.190 = f32[16896,3]{1,0:T(8,128)} copy(f32[16896,3]{0,1:T(4,128)S(1)} %maximum_bitcast_fusion) | data formatting | bytes 405504 | tf_op jit(solution)/shard_map/transpose | solution.py:130
  267.3 90.4 %scatter_custom_fusion.3 = f32[576,3]{1,0:T(8,128)S(1)} fusion(s32[16896]{0:T(1024)S(1)} %pad_add_fusion, f32[16896,3]{1,0:T(8,128)} %copy.190, f32[]{:T(128)} %constant.196.clone.1), kind=kCustom, calls=%fused_computation.32 | custom fusion | flops 50688 | bytes 7424 | tf_op jit(solution)/shard_map/scatter-add | solution.py:130
  357.9 5.7 %collective-permute-start.13 = (f32[3,1,1,9,64]{4,2,3,1,0:T(1,128)S(1)}, f32[3,1,1,9,64]{4,2,3,1,0:T(1,128)S(1)}, u32[]{:S(2)}, u32[]{:S(2)}) collective-permute-start(f32[3,1,1,9,64]{4,2,3,1,0:T(1,128)S(1)} %copy.191), channel_id=1, source_target_pairs={{16,0},{32,16},{48,32},{64,48},{80,64},{96,80},{112,96},{128,112},... | collective-permute-start | bytes 20744 | tf_op jit(solution)/shard_map/ppermute | solution.py:54
  364.4 5.3 %collective-permute-done.12 = f32[3,1,1,9,64]{4,2,3,1,0:T(1,128)S(1)} collective-permute-done((f32[3,1,1,9,64]{4,2,3,1,0:T(1,128)S(1)}, f32[3,1,1,9,64]{4,2,3,1,0:T(1,128)S(1)}, u32[]{:S(2)}, u32[]{:S(2)}) %collective-permute-start.12) | collective-permute-done | bytes 6944 | tf_op jit(solution)/shard_map/ppermute | solution.py:51
  369.8 3.0 collective-permute-start.15
  373.6 1.7 collective-permute-done.14
  375.5 3.9 collective-permute-done.2
  379.5 3.7 collective-permute-start.3
  384.0 3.7 collective-permute-done.3
  389.6 3.0 collective-permute-start.4
  393.8 1.1 collective-permute-done.5
  394.9 2.5 collective-permute-done.4
  397.8 2.6 collective-permute-start.6
  400.5 1.0 collective-permute-start.7
  402.2 2.2 collective-permute-done.7
  405.6 60.6 %scatter_fusion.2 = f32[155648]{0:T(1024)S(1)} fusion(f32[155648]{0:T(1024)S(1)} %bitcast.399, s32[16384]{0:T(1024)S(1)} %bitcast.440, f32[16384]{0:T(1024)S(1)} %multiply_subtract_fusion), kind=kCustom, calls=%fused_computation.10 | custom fusion | bytes 262144 | tf_op jit(solution)/shard_map/scatter | solution.py:119
  466.2 0.8 copy-done
  (139 shorter events, 13.8 us)
Async XLA Ops:
  0.6 31.8 %copy-start.3 = (s32[1,1,16384]{2,1,0:T(1,128)S(1)}, s32[1,1,16384]{2,1,0:T(1,128)}, u32[]{:S(2)}) copy-start(s32[1,1,16384]{2,1,0:T(1,128)} %param.24) | copy-start | bytes 196612
  0.6 31.9 %copy-start.4 = (s32[1,1,16384]{2,1,0:T(1,128)S(1)}, s32[1,1,16384]{2,1,0:T(1,128)}, u32[]{:S(2)}) copy-start(s32[1,1,16384]{2,1,0:T(1,128)} %param.22) | copy-start | bytes 196612
  0.7 31.9 %copy-start.2 = (s32[1,1,16384]{2,1,0:T(1,128)S(1)}, s32[1,1,16384]{2,1,0:T(1,128)}, u32[]{:S(2)}) copy-start(s32[1,1,16384]{2,1,0:T(1,128)} %param.23) | copy-start | bytes 196612
  0.7 104.1 %collective-permute-start.8 = (f32[3,1,1,64]{3,2,1,0:T(1,128)}, f32[3,1,1,64]{3,2,1,0:T(1,128)S(1)}, u32[]{:S(2)}, u32[]{:S(2)}) collective-permute-start(f32[3,1,1,64]{3,2,1,0:T(1,128)} %param.21), channel_id=1, source_target_pairs={{0,16},{16,32},{32,48},{48,64},{64,80},{80,96},{96,112},{112,128},... | collective-permute-start | bytes 2312 | tf_op jit(solution)/shard_map/ppermute | solution.py:51
  4.3 100.5 %collective-permute-start.9 = (f32[3,1,1,64]{3,2,1,0:T(1,128)}, f32[3,1,1,64]{3,2,1,0:T(1,128)S(1)}, u32[]{:S(2)}, u32[]{:S(2)}) collective-permute-start(f32[3,1,1,64]{3,2,1,0:T(1,128)} %param.21), channel_id=1, source_target_pairs={{16,0},{32,16},{48,32},{64,48},{80,64},{96,80},{112,96},{128,112},... | collective-permute-start | bytes 2312 | tf_op jit(solution)/shard_map/ppermute | solution.py:54
  26.5 337.1 %collective-permute-start = (f32[4,5,8,128]{3,2,1,0:T(8,128)S(1)}, f32[4,5,8,128]{3,2,1,0:T(8,128)S(1)}, u32[]{:S(2)}, u32[]{:S(2)}) collective-permute-start(f32[4,5,8,128]{3,2,1,0:T(8,128)S(1)} %pad_maximum_fusion.7), channel_id=1, source_target_pairs={{240,0},{0,16},{16,32},{32,48},{48,64},{64,80},{80,96},{96,112},{1... | collective-permute-start | bytes 245768 | tf_op jit(solution)/shard_map/ppermute | solution.py:42
  33.0 65.0 %copy-start.14 = (f32[4,19]{1,0:T(4,128)S(1)}, f32[4,19]{1,0:T(4,128)}, u32[]{:S(2)}) copy-start(f32[4,19]{1,0:T(4,128)} %constant.236.clone) | copy-start | bytes 916
  89.6 14.3 %copy-start.8 = (s32[1,1,256]{2,1,0:T(1,128)S(1)}, s32[1,1,256]{2,1,0:T(1,128)}, u32[]{:S(2)}) copy-start(s32[1,1,256]{2,1,0:T(1,128)} %param.26) | copy-start | bytes 3076
  89.6 14.9 %copy-start.11 = (f32[1,1,256]{2,1,0:T(1,128)S(1)}, f32[1,1,256]{2,1,0:T(1,128)}, u32[]{:S(2)}) copy-start(f32[1,1,256]{2,1,0:T(1,128)} %param.29) | copy-start | bytes 3076
  89.6 15.0 %copy-start.7 = (s32[1,1,256]{2,1,0:T(1,128)S(1)}, s32[1,1,256]{2,1,0:T(1,128)}, u32[]{:S(2)}) copy-start(s32[1,1,256]{2,1,0:T(1,128)} %param.27) | copy-start | bytes 3076
  89.6 15.0 %copy-start.1 = (f32[19,8,8,128]{3,2,1,0:T(8,128)S(1)}, f32[19,8,8,128]{3,2,1,0:T(8,128)}, u32[]{:S(2)}) copy-start(f32[19,8,8,128]{3,2,1,0:T(8,128)} %param.19) | copy-start | bytes 1867780
  89.6 15.2 %copy-start.6 = (f32[3,1,1,64]{3,2,1,0:T(1,128)S(1)}, f32[3,1,1,64]{3,2,1,0:T(1,128)}, u32[]{:S(2)}) copy-start(f32[3,1,1,64]{3,2,1,0:T(1,128)} %param.21) | copy-start | bytes 2308
  104.8 95.2 %collective-permute-start.11 = (f32[3,3,1,64]{3,2,1,0:T(1,128)S(1)}, f32[3,3,1,64]{3,2,1,0:T(1,128)S(1)}, u32[]{:S(2)}, u32[]{:S(2)}) collective-permute-start(f32[3,3,1,64]{3,2,1,0:T(1,128)S(1)} %constant_dynamic-update-slice_fusion.35), channel_id=1, source_target_pairs={{1,0},{2,1},{3,2},{4,3},{5,4},{6,5},{7,6},{8,7},{9,8},{10,9},{11,1... | collective-permute-start | bytes 6920 | tf_op jit(solution)/shard_map/ppermute | solution.py:54
  105.9 94.2 %collective-permute-start.10 = (f32[3,3,1,64]{3,2,1,0:T(1,128)S(1)}, f32[3,3,1,64]{3,2,1,0:T(1,128)S(1)}, u32[]{:S(2)}, u32[]{:S(2)}) collective-permute-start(f32[3,3,1,64]{3,2,1,0:T(1,128)S(1)} %constant_dynamic-update-slice_fusion.35), channel_id=1, source_target_pairs={{0,1},{1,2},{2,3},{3,4},{4,5},{5,6},{6,7},{7,8},{8,9},{9,10},{10,1... | collective-permute-start | bytes 6920 | tf_op jit(solution)/shard_map/ppermute | solution.py:51
  200.0 62.0 %copy-start.5 = (f32[3,1,1,256]{3,2,1,0:T(1,128)S(1)}, f32[3,1,1,256]{3,2,1,0:T(1,128)}, u32[]{:S(2)}) copy-start(f32[3,1,1,256]{3,2,1,0:T(1,128)} %param.30) | copy-start | bytes 9220
  260.1 127.7 %copy-start.13 = (f32[5]{0:T(128)S(1)}, f32[5]{0:T(128)}, u32[]{:S(2)}) copy-start(f32[5]{0:T(128)} %constant.256) | copy-start | bytes 64
  260.1 127.7 %copy-start.10 = (s32[5]{0:T(128)S(1)}, s32[5]{0:T(128)}, u32[]{:S(2)}) copy-start(s32[5]{0:T(128)} %constant.271) | copy-start | bytes 64
  260.2 128.4 %copy-start.12 = (f32[5]{0:T(128)S(1)}, f32[5]{0:T(128)}, u32[]{:S(2)}) copy-start(f32[5]{0:T(128)} %constant.235.clone) | copy-start | bytes 64
  260.2 128.5 %copy-start.9 = (s32[5]{0:T(128)S(1)}, s32[5]{0:T(128)}, u32[]{:S(2)}) copy-start(s32[5]{0:T(128)} %constant.270) | copy-start | bytes 64
  357.9 6.5 %collective-permute-start.13 = (f32[3,1,1,9,64]{4,2,3,1,0:T(1,128)S(1)}, f32[3,1,1,9,64]{4,2,3,1,0:T(1,128)S(1)}, u32[]{:S(2)}, u32[]{:S(2)}) collective-permute-start(f32[3,1,1,9,64]{4,2,3,1,0:T(1,128)S(1)} %copy.191), channel_id=1, source_target_pairs={{16,0},{32,16},{48,32},{64,48},{80,64},{96,80},{112,96},{128,112},... | collective-permute-start | bytes 20744 | tf_op jit(solution)/shard_map/ppermute | solution.py:54
  363.6 6.2 %collective-permute-start.12 = (f32[3,1,1,9,64]{4,2,3,1,0:T(1,128)S(1)}, f32[3,1,1,9,64]{4,2,3,1,0:T(1,128)S(1)}, u32[]{:S(2)}, u32[]{:S(2)}) collective-permute-start(f32[3,1,1,9,64]{4,2,3,1,0:T(1,128)S(1)} %copy.191), channel_id=1, source_target_pairs={{0,16},{16,32},{32,48},{48,64},{64,80},{80,96},{96,112},{112,128},... | collective-permute-start | bytes 20744 | tf_op jit(solution)/shard_map/ppermute | solution.py:51
  363.7 9.1 %collective-permute-start.1 = (f32[4,5,8,128]{3,2,1,0:T(8,128)S(1)}, f32[4,5,8,128]{3,2,1,0:T(8,128)S(1)}, u32[]{:S(2)}, u32[]{:S(2)}) collective-permute-start(f32[4,5,8,128]{3,2,1,0:T(8,128)S(1)} %broadcast_select_fusion), channel_id=1, source_target_pairs={{224,0},{240,16},{0,32},{16,48},{32,64},{48,80},{64,96},{80,112},{... | collective-permute-start | bytes 245768 | tf_op jit(solution)/shard_map/ppermute | solution.py:42
  369.8 3.8 collective-permute-start.15
  372.7 2.5 collective-permute-start.14
  372.8 6.6 %collective-permute-start.2 = (f32[4,5,8,128]{3,2,1,0:T(8,128)S(1)}, f32[4,5,8,128]{3,2,1,0:T(8,128)S(1)}, u32[]{:S(2)}, u32[]{:S(2)}) collective-permute-start(f32[4,5,8,128]{3,2,1,0:T(8,128)S(1)} %broadcast_select_fusion.1), channel_id=1, source_target_pairs={{192,0},{208,16},{224,32},{240,48},{0,64},{16,80},{32,96},{48,112}... | collective-permute-start | bytes 245768 | tf_op jit(solution)/shard_map/ppermute | solution.py:42
  379.5 8.2 %collective-permute-start.3 = (f32[4,5,8,128]{3,2,1,0:T(8,128)S(1)}, f32[4,5,8,128]{3,2,1,0:T(8,128)S(1)}, u32[]{:S(2)}, u32[]{:S(2)}) collective-permute-start(f32[4,5,8,128]{3,2,1,0:T(8,128)S(1)} %broadcast_select_fusion.2), channel_id=1, source_target_pairs={{128,0},{144,16},{160,32},{176,48},{192,64},{208,80},{224,96},{240... | collective-permute-start | bytes 245768 | tf_op jit(solution)/shard_map/ppermute | solution.py:42
  389.5 5.4 %collective-permute-start.5 = (f32[16,1,10,128]{3,2,1,0:T(8,128)S(1)}, f32[16,1,10,128]{3,2,1,0:T(8,128)S(1)}, u32[]{:S(2)}, u32[]{:S(2)}) collective-permute-start(f32[16,1,10,128]{3,2,1,0:T(8,128)S(1)} %get-tuple-element.77), channel_id=1, source_target_pairs={{16,0},{32,16},{48,32},{64,48},{80,64},{96,80},{112,96},{128,112},... | collective-permute-start | bytes 245768 | tf_op jit(solution)/shard_map/ppermute | solution.py:54
  389.6 7.8 %collective-permute-start.4 = (f32[16,1,10,128]{3,2,1,0:T(8,128)S(1)}, f32[16,1,10,128]{3,2,1,0:T(8,128)S(1)}, u32[]{:S(2)}, u32[]{:S(2)}) collective-permute-start(f32[16,1,10,128]{3,2,1,0:T(8,128)S(1)} %get-tuple-element.78), channel_id=1, source_target_pairs={{0,16},{16,32},{32,48},{48,64},{64,80},{80,96},{96,112},{112,128},... | collective-permute-start | bytes 245768 | tf_op jit(solution)/shard_map/ppermute | solution.py:51
  397.8 4.3 collective-permute-start.6
  400.5 3.9 collective-permute-start.7
  466.2 0.8 copy-start
where the time goes:
time: 471 us; the launch traced here: 467 us
  local copies, waits for them, and re-layouts  285 us (61%)
  other arithmetic  118 us (25%)
  starting transfers between devices  30.1 us (6%)
  waiting for transfers between devices  22.1 us (5%)
  between operations  5.89 us (1%)
  matrix products  5.84 us (1%)
    gather x1, local copies, waits for them, and re-layouts, tile_links(): bounced = leaving - 6.0 * picked[3] * density[link_cell] * c_dot_u  90.5 us
    scatter-add x1, other arithmetic, tile_links(): jax.ops.segment_sum(values.T, sphere_refs, num_segments=9 * slot_count)  90.4 us
    scatter x1, local copies, waits for them, and re-layouts, tile_links(): propagated.reshape(-1).at[target].set(bounced, mode='drop')  60.6 us
    gather x2, local copies, waits for them, and re-layouts, tile_links(): wall_speed = near_speed[:, link_sphere]  59.8 us
    gather x1, local copies, waits for them, and re-layouts, tile_links(): leaving = jnp.sum(onehot * relaxed[:, link_cell], axis=0)  56.6 us
    ppermute x6, starting transfers between devices, padded(): lax.ppermute(lax.slice_in_dim(block, 0, width, axis=dim), axis, backward)  16.2 us
    unnamed x28, other arithmetic  12.6 us
    ppermute x6, starting transfers between devices, padded(): lax.ppermute(lax.slice_in_dim(block, block.shape[dim] - width, None, axis...  10 us
  transfers between devices with their start and end apart: 16, of which 10 were waited for; matrix products, arithmetic and copies ran while one was open for 74% of the time, Pallas kernels for 0%

commit v1 on v0

v1 whole, which is shorter than its diff:
```python
import functools

import jax
import jax.numpy as jnp
from jax import lax
from jax.experimental import pallas as pl
from jax.experimental.pallas import tpu as pltpu
from jax.sharding import PartitionSpec as P

MESH = pl.DeviceIdType.MESH
VELOCITIES = [
    (0, 0, 0),
    (1, 0, 0),
    (-1, 0, 0),
    (0, 1, 0),
    (0, -1, 0),
    (0, 0, 1),
    (0, 0, -1),
    (1, 1, 0),
    (-1, -1, 0),
    (1, -1, 0),
    (-1, 1, 0),
    (1, 0, 1),
    (-1, 0, -1),
    (1, 0, -1),
    (-1, 0, 1),
    (0, 1, 1),
    (0, -1, -1),
    (0, 1, -1),
    (0, -1, 1),
]
WEIGHTS = [1.0 / 3.0] + [1.0 / 18.0] * 6 + [1.0 / 36.0] * 12
UPWARD = [3, 7, 10, 15, 17]
DOWNWARD = [4, 8, 9, 16, 18]
RIGHTWARD = [1, 7, 9, 11, 13]
LEFTWARD = [2, 8, 10, 12, 14]
RELAX_TIME = 0.8
SHEAR_SPEED = 0.1
LUB_COEF = 0.5
GAP_FLOOR = 0.1
GAP_CUTOFF = 1.0
INV_MASS = 1.0 / 523.6

LANES = 128
ROWS = 18 * 64
PAD = 64
REF_BITS = 10
DEAD = 1 << 30
LINK_ROWS = 128
SUM_ROWS = LINK_ROWS + 8


def iota(shape, dim):
    return lax.broadcasted_iota(jnp.int32, shape, dim)


def take(table, lanes):
    return jnp.take_along_axis(table, lanes, axis=1, mode="promise_in_bounds")


def collide(current):
    density = current[0]
    for direction in range(1, 19):
        density = density + current[direction]
    inverse = 1.0 / density
    speeds = []
    for axis_id in range(3):
        running = None
        for direction, vector in enumerate(VELOCITIES):
            if vector[axis_id] == 0:
                continue
            value = current[direction]
            if running is None:
                running = value
            elif vector[axis_id] > 0:
                running = running + value
            else:
                running = running - value
        speeds.append(running * inverse)
    speed_sq = speeds[0] * speeds[0] + speeds[1] * speeds[1] + speeds[2] * speeds[2]
    common = 1.0 - 1.5 * speed_sq
    kept = 1.0 - 1.0 / RELAX_TIME
    relaxed = [kept * current[0] + (WEIGHTS[0] / RELAX_TIME) * density * common]
    scaled = {}
    for direction in range(1, 19, 2):
        vector = VELOCITIES[direction]
        weight = WEIGHTS[direction]
        if weight not in scaled:
            scaled[weight] = (weight / RELAX_TIME) * density
        c_dot = None
        for axis_id in range(3):
            if vector[axis_id] != 0:
                term = speeds[axis_id]
                if c_dot is None:
                    c_dot = term
                elif vector[axis_id] > 0:
                    c_dot = c_dot + term
                else:
                    c_dot = c_dot - term
        even = scaled[weight] * (common + 4.5 * c_dot * c_dot)
        odd = scaled[weight] * (3.0 * c_dot)
        relaxed.append(kept * current[direction] + (even + odd))
        relaxed.append(kept * current[direction + 1] + (even - odd))
    return relaxed, density


def bitonic_sort(keys):
    place = iota((16, 8, 128), 0) + 16 * iota((16, 8, 128), 1) + 128 * iota((16, 8, 128), 2)
    sublane = iota((16, 8, 128), 1)
    lane = iota((128, 128), 1)
    for phase in range(1, 15):
        flips = place >> (phase - 1)
        if phase == 1:
            flips = place >> 1
        elif phase < 14:
            flips = flips ^ (place >> phase)
        keys = keys ^ (-(flips & 1))
        for bit in range(phase - 1, -1, -1):
            if bit < 4:
                step = 1 << bit
                pairs = keys.reshape(8 >> bit, 2, step, 8, 128)
                first, second = pairs[:, 0], pairs[:, 1]
                low, high = jnp.minimum(first, second), jnp.maximum(first, second)
                keys = jnp.stack([low, high], axis=1).reshape(16, 8, 128)
            elif bit < 7:
                step = 1 << (bit - 4)
                upper = (sublane & step) != 0
                partner = pltpu.roll(keys, step, 1)
                if step != 4:
                    partner = jnp.where(upper, partner, pltpu.roll(keys, 8 - step, 1))
                keys = jnp.where(upper, jnp.maximum(keys, partner), jnp.minimum(keys, partner))
            else:
                step = 1 << (bit - 7)
                flat = keys.reshape(128, 128)
                partner = take(flat, lane ^ step)
                upper = (lane & step) != 0
                flat = jnp.where(upper, jnp.maximum(flat, partner), jnp.minimum(flat, partner))
                keys = flat.reshape(16, 8, 128)
    return keys


def step_kernel(
    n_flow,
    n_grad,
    offset_ref,
    link_count_ref,
    pair_count_ref,
    pop_ref,
    velocity_ref,
    cell_ref,
    dir_ref,
    sphere_ref,
    first_ref,
    second_ref,
    gap_ref,
    normal_ref,
    next_ref,
    force_ref,
    moved_ref,
    relaxed,
    density,
    face_right,
    face_left,
    face_up,
    face_down,
    from_left,
    from_right,
    from_below,
    from_above,
    own_speed,
    near,
    speed_rows,
    sorted_keys,
    spread,
    strength,
    pair_ints,
    pair_floats,
    sum_code,
    sum_slot,
    sum_piece,
    part_out,
    part_in,
    face_send,
    face_recv,
    up_send,
    up_recv,
    down_send,
    down_recv,
    speed_send,
    speed_recv,
    part_send,
    part_recv,
):
    flow, grad = lax.axis_index("flow"), lax.axis_index("grad")
    right, left = lax.rem(flow + 1, n_flow), lax.rem(flow + n_flow - 1, n_flow)
    above, below = lax.rem(grad + 1, n_grad), lax.rem(grad + n_grad - 1, n_grad)
    up_targets = jnp.where(grad == n_grad - 1, n_flow, 3)
    down_targets = jnp.where(grad == 0, n_flow, 3)

    def column(step):
        return lax.rem(flow + n_flow - 1 + step, n_flow)

    barrier = pltpu.get_barrier_semaphore()
    for target in (left, right):
        pl.semaphore_signal(barrier, inc=1, device_id=(target, grad), device_id_type=MESH)

    def greet_up(step, carry):
        pl.semaphore_signal(barrier, inc=1, device_id=(column(step), above), device_id_type=MESH)
        return carry

    def greet_down(step, carry):
        pl.semaphore_signal(barrier, inc=1, device_id=(column(step), below), device_id_type=MESH)
        return carry

    lax.fori_loop(0, up_targets, greet_up, 0)
    lax.fori_loop(0, down_targets, greet_down, 0)

    for axis_id in range(3):
        own_speed[axis_id : axis_id + 1, 0:64] = velocity_ref[axis_id, 0]

    def collide_slab(x, carry):
        rows = pl.ds(pl.multiple_of(x * 8, 8), 8)
        values, total = collide([pop_ref[direction, x] for direction in range(19)])
        for direction in range(19):
            relaxed[direction, rows, :] = values[direction]
        density[rows, :] = total
        return carry

    lax.fori_loop(0, 8, collide_slab, 0)
    for slot in range(5):
        face_right[slot] = relaxed[RIGHTWARD[slot], 56:64, :]
        face_left[slot] = relaxed[LEFTWARD[slot], 0:8, :]
        face_up[slot] = relaxed[UPWARD[slot], pl.ds(7, 8, stride=8), :]
        face_down[slot] = relaxed[DOWNWARD[slot], pl.ds(0, 8, stride=8), :]

    pl.semaphore_wait(barrier, 2 + up_targets + down_targets)

    def speed_copy(code):
        target = (
            lax.rem(flow + n_flow - (code // 3 - 1), n_flow),
            lax.rem(grad + n_grad - (code % 3 - 1), n_grad),
        )
        return pltpu.make_async_remote_copy(
            src_ref=own_speed,
            dst_ref=near.at[code],
            send_sem=speed_send.at[code],
            recv_sem=speed_recv.at[code],
            device_id=target,
            device_id_type=MESH,
        )

    def part_copy(code):
        target = (
            lax.rem(flow + n_flow + (code // 3 - 1), n_flow),
            lax.rem(grad + n_grad + (code % 3 - 1), n_grad),
        )
        return pltpu.make_async_remote_copy(
            src_ref=part_out.at[code],
            dst_ref=part_in.at[code],
            send_sem=part_send.at[code],
            recv_sem=part_recv.at[code],
            device_id=target,
            device_id_type=MESH,
        )

    neighbours = [code for code in range(9) if code != 4]

    def face_copies():
        return (
            pltpu.make_async_remote_copy(
                src_ref=face_right,
                dst_ref=from_left,
                send_sem=face_send.at[0],
                recv_sem=face_recv.at[0],
                device_id=(right, grad),
                device_id_type=MESH,
            ),
            pltpu.make_async_remote_copy(
                src_ref=face_left,
                dst_ref=from_right,
                send_sem=face_send.at[1],
                recv_sem=face_recv.at[1],
                device_id=(left, grad),
                device_id_type=MESH,
            ),
        )

    def up_copy(target, source):
        return pltpu.make_async_remote_copy(
            src_ref=face_up,
            dst_ref=from_below.at[:, pl.ds(pl.multiple_of(source * 8, 8), 8), :],
            send_sem=up_send.at[target],
            recv_sem=up_recv.at[source],
            device_id=(target, above),
            device_id_type=MESH,
        )

    def down_copy(target, source):
        return pltpu.make_async_remote_copy(
            src_ref=face_down,
            dst_ref=from_above.at[:, pl.ds(pl.multiple_of(source * 8, 8), 8), :],
            send_sem=down_send.at[target],
            recv_sem=down_recv.at[source],
            device_id=(target, below),
            device_id_type=MESH,
        )

    def send_up(step, carry):
        up_copy(column(step), flow).start()
        return carry

    def send_down(step, carry):
        down_copy(column(step), flow).start()
        return carry

    lax.fori_loop(0, up_targets, send_up, 0)
    lax.fori_loop(0, down_targets, send_down, 0)
    for copy in face_copies():
        copy.start()
    for code in neighbours:
        speed_copy(code).start()

    number = iota((128, 128), 0) * 128 + iota((128, 128), 1)
    packed = (((dir_ref[...] - 1) * 8192 + cell_ref[...]) << REF_BITS) + sphere_ref[...]
    packed = jnp.where(number < link_count_ref[0, 0], packed, DEAD)
    ordered = bitonic_sort(packed.reshape(16, 8, 128))
    sorted_keys[...] = ordered.reshape(128, 128)
    picked = [sorted_keys[pl.ds(sublane, 16, stride=8), :] for sublane in range(8)]
    natural = jnp.transpose(jnp.concatenate(picked, axis=0))
    sorted_keys[...] = natural
    lag = natural - (number << REF_BITS)
    rest = lag & ((1 << 24) - 1)
    home = lag >> 24
    nothing = jnp.full((PAD, 128), -1, jnp.int32)
    for level in range(15):
        spread[level, 0:PAD, :] = nothing
    for block in range(9):
        spread[14, PAD + block * 128 : PAD + block * 128 + 128, :] = jnp.where(home == block, rest, -1)
    lane = iota((128, 128), 1)

    def spread_level(bit):
        unit = 1 << (bit + REF_BITS)

        def block_of(block, carry):
            base = pl.multiple_of(block * 128, 128)
            here = spread[bit + 1, pl.ds(base + PAD, 128), :]
            if bit >= 7:
                coming = spread[bit + 1, pl.ds(base + (PAD - (1 << (bit - 7))), 128), :]
            else:
                before = spread[bit + 1, pl.ds(base + (PAD - 1), 128), :]
                coming = pltpu.roll(jnp.where(lane >= 128 - (1 << bit), before, here), 1 << bit, 1)
            stays = jnp.where(here < unit, here, -1)
            spread[bit, pl.ds(base + PAD, 128), :] = jnp.where(coming >= unit, coming - unit, stays)
            return carry

        lax.fori_loop(0, 9, block_of, 0)

    for bit in range(13, -1, -1):
        spread_level(bit)

    for code in neighbours:
        speed_copy(code).wait_recv()
    near[4] = own_speed[...]
    half = iota((8, 128), 1) < 64
    for pair in range(5):
        row = near[2 * pair]
        if pair < 4:
            row = jnp.where(half, row, pltpu.roll(near[2 * pair + 1], 64, 1))
        for axis_id in range(3):
            speed_rows[45 + 5 * axis_id + pair : 46 + 5 * axis_id + pair, :] = row[axis_id : axis_id + 1]
        for line in range(9):
            vector = VELOCITIES[2 * line + 1]
            total = None
            for axis_id in range(3):
                if vector[axis_id] != 0:
                    term = row[axis_id : axis_id + 1]
                    if total is None:
                        total = term
                    elif vector[axis_id] > 0:
                        total = total + term
                    else:
                        total = total - term
            speed_rows[5 * line + pair : 5 * line + pair + 1, :] = total

    def speed_of(line, refs):
        lanes = refs & 127
        group = refs >> 7
        found = take(jnp.broadcast_to(speed_rows[5 * line : 5 * line + 1, :], refs.shape), lanes)
        for pair in range(1, 5):
            row = jnp.broadcast_to(speed_rows[5 * line + pair : 5 * line + pair + 1, :], refs.shape)
            found = jnp.where(group == pair, take(row, lanes), found)
        return found

    def came_up(step, carry):
        up_copy(column(step), column(step)).wait_recv()
        return carry

    def came_down(step, carry):
        down_copy(column(step), column(step)).wait_recv()
        return carry

    lax.fori_loop(0, down_targets, came_up, 0)
    lax.fori_loop(0, up_targets, came_down, 0)
    for copy in face_copies():
        copy.wait_recv()

    span = 8 * n_flow
    offset = offset_ref[0]
    at_bottom, at_top = grad == 0, grad == n_grad - 1
    shift_below = jnp.where(at_bottom, offset, 0)
    shift_above = jnp.where(at_top, span - offset, 0)
    boost_below = jnp.where(at_bottom, -6.0 * SHEAR_SPEED, 0.0)
    boost_above = jnp.where(at_top, 6.0 * SHEAR_SPEED, 0.0)
    tall = iota((8, 128), 0)

    def propagated(direction):
        c_x, c_y, c_z = VELOCITIES[direction]
        slabs = []
        for x in range(8):
            source = x - c_x
            if c_x == 0 or 0 <= source < 8:
                slab = relaxed[direction, source * 8 : source * 8 + 8, :]
            elif c_x > 0:
                slab = from_left[RIGHTWARD.index(direction)]
            else:
                slab = from_right[LEFTWARD.index(direction)]
            if c_y != 0:
                rows_from, shift, boost = (from_below, shift_below, boost_below) if c_y > 0 else (from_above, shift_above, boost_above)
                slot = (UPWARD if c_y > 0 else DOWNWARD).index(direction)
                place = lax.rem(flow * 8 + (source + span) + shift, span)
                ghost = rows_from[slot, pl.ds(place, 1), :]
                if c_x != 0:
                    ghost = ghost + boost * (WEIGHTS[direction] * c_x)
                slab = pltpu.roll(slab, 1 if c_y > 0 else 7, 0)
                slab = jnp.where(tall == (0 if c_y > 0 else 7), jnp.broadcast_to(ghost, (8, 128)), slab)
            if c_z != 0:
                slab = pltpu.roll(slab, 1 if c_z > 0 else 127, 1)
            slabs.append(slab)
        return jnp.concatenate(slabs, axis=0)

    next_ref[0] = relaxed[0].reshape(8, 8, 128)
    for direction in range(1, 19):
        opposite = direction + 1 if direction % 2 == 1 else direction - 1
        sign = 1.0 if direction % 2 == 1 else -1.0
        refs = spread[0, PAD + 64 * (direction - 1) : PAD + 64 * direction, :]
        leaving = relaxed[direction]
        wall = speed_of((direction - 1) // 2, refs)
        bounced = leaving - (6.0 * WEIGHTS[direction] * sign) * density[...] * wall
        strength[0, 64 * (direction - 1) : 64 * direction, :] = leaving + bounced
        updated = jnp.where(refs >= 0, bounced, propagated(opposite))
        next_ref[opposite] = updated.reshape(8, 8, 128)

    def gather_level(bit):
        unit = 1 << (bit + REF_BITS)
        now, later = bit % 2, (bit + 1) % 2

        def block_of(block, carry):
            base = pl.multiple_of(block * 128, 128)
            moves = spread[bit + 1, pl.ds(base + PAD, 128), :] >= unit
            here = strength[now, pl.ds(base, 128), :]
            if bit >= 7:
                ahead = strength[now, pl.ds(base + (1 << (bit - 7)), 128), :]
            else:
                after = strength[now, pl.ds(base + 1, 128), :]
                ahead = pltpu.roll(jnp.where(lane < (1 << bit), after, here), 128 - (1 << bit), 1)
            strength[later, pl.ds(base, 128), :] = jnp.where(moves, ahead, here)
            return carry

        lax.fori_loop(0, 9, block_of, 0)

    for bit in range(14):
        gather_level(bit)
    keys = sorted_keys[...]
    lag = keys - (number << REF_BITS)
    home = lag >> 24
    push = jnp.zeros((128, 128), jnp.float32)
    for block in range(9):
        push = jnp.where(home == block, strength[0, block * 128 : block * 128 + 128, :], push)

    def put_terms(rows, refs, terms):
        sum_code[rows, :] = refs >> 6
        sum_slot[rows, :] = refs & 63
        for axis_id in range(3):
            coarse = terms[axis_id].astype(jnp.bfloat16).astype(jnp.float32)
            sum_piece[axis_id, rows, :] = coarse
            sum_piece[3 + axis_id, rows, :] = terms[axis_id] - coarse

    kind = (keys >> 23) & 127
    small_lane = iota((8, 128), 1)
    terms = []
    for axis_id in range(3):
        table = jnp.zeros((8, 128), jnp.float32)
        for direction in range(1, 19):
            part = VELOCITIES[direction][axis_id]
            if part != 0:
                table = jnp.where(small_lane == direction - 1, float(part), table)
        tall_table = jnp.concatenate([table] * 16, axis=0)
        terms.append(take(tall_table, kind) * push)
    put_terms(pl.ds(0, 128), keys & 1023, terms)

    pair_ints[...] = jnp.zeros((2, 8, 128), jnp.int32)
    pair_floats[...] = jnp.ones((4, 8, 128), jnp.float32)
    for row in range(2):
        lanes = slice(row * 128, row * 128 + 128)
        pair_ints[0, row : row + 1, :] = first_ref[0, :, lanes] + 256
        pair_ints[1, row : row + 1, :] = second_ref[0, :, lanes]
        pair_floats[3, row : row + 1, :] = gap_ref[0, :, lanes]
        for axis_id in range(3):
            pair_floats[axis_id, row : row + 1, :] = normal_ref[axis_id, 0, :, lanes]
    heads, tails = pair_ints[0], pair_ints[1]
    normals = [pair_floats[axis_id] for axis_id in range(3)]
    rate = None
    for axis_id in range(3):
        gap_speed = (speed_of(9 + axis_id, heads) - speed_of(9 + axis_id, tails)) * normals[axis_id]
        rate = gap_speed if rate is None else rate + gap_speed
    resist = LUB_COEF * (1.0 / jnp.maximum(pair_floats[3], GAP_FLOOR) - 1.0 / GAP_CUTOFF)
    alive = iota((8, 128), 0) * 128 + small_lane < jnp.minimum(pair_count_ref[0, 0], 256)
    scale = jnp.where(alive, -resist * rate, 0.0)
    lift = [scale * normals[axis_id] for axis_id in range(3)]
    lower = iota((8, 128), 0) < 2
    both = jnp.where(lower, heads, pltpu.roll(tails, 2, 0))
    lift = [jnp.where(lower, term, -pltpu.roll(term, 2, 0)) for term in lift]
    put_terms(pl.ds(128, 8), both, lift)

    code_rows = iota((16, 128), 0)
    slot_rows = iota((64, 128), 0)

    def add_rows(group, total):
        base = group * 8
        pieces, slots = [], []
        for row in range(8):
            at = pl.ds(base + row, 1)
            chosen = code_rows == jnp.broadcast_to(sum_code[at, :], (16, 128))
            parts = [
                jnp.where(chosen, jnp.broadcast_to(sum_piece[piece, at, :], (16, 128)), 0.0).astype(jnp.bfloat16)
                for piece in range(6)
            ]
            pieces.append(jnp.concatenate(parts, axis=0))
            slot = slot_rows == jnp.broadcast_to(sum_slot[at, :], (64, 128))
            slots.append(jnp.where(slot, 1.0, 0.0).astype(jnp.bfloat16))
        return total + lax.dot_general(
            jnp.concatenate(pieces, axis=1),
            jnp.concatenate(slots, axis=1),
            (((1,), (1,)), ((), ())),
            preferred_element_type=jnp.float32,
        )

    total = lax.fori_loop(0, SUM_ROWS // 8, add_rows, jnp.zeros((96, 64), jnp.float32))
    for axis_id in range(3):
        summed = total[16 * axis_id : 16 * axis_id + 16] + total[48 + 16 * axis_id : 64 + 16 * axis_id]
        for code in range(9):
            part_out[code, axis_id : axis_id + 1, 0:64] = summed[code : code + 1]

    for code in neighbours:
        part_copy(code).start()
    forces = part_out[4]
    for code in neighbours:
        part_copy(code).wait_recv()
        forces = forces + part_in[code]
    for axis_id in range(3):
        force = forces[axis_id : axis_id + 1, 0:64]
        force_ref[axis_id, 0] = force
        moved_ref[axis_id, 0] = velocity_ref[axis_id, 0] + INV_MASS * force

    for code in neighbours:
        part_copy(code).wait_send()
        speed_copy(code).wait_send()
    for copy in face_copies():
        copy.wait_send()

    def sent_up(step, carry):
        up_copy(column(step), flow).wait_send()
        return carry

    def sent_down(step, carry):
        down_copy(column(step), flow).wait_send()
        return carry

    lax.fori_loop(0, up_targets, sent_up, 0)
    lax.fori_loop(0, down_targets, sent_down, 0)


def per_device(
    n_flow,
    n_grad,
    populations,
    le_offset,
    sphere_velocity,
    link_cell,
    link_dir,
    link_sphere,
    link_count,
    pair_first,
    pair_second,
    pair_count,
    pair_gap,
    pair_normal,
):
    vmem = pl.BlockSpec(memory_space=pltpu.VMEM)
    smem = pl.BlockSpec(memory_space=pltpu.SMEM)
    span = 8 * n_flow
    f32, i32 = jnp.float32, jnp.int32
    dma = pltpu.SemaphoreType.DMA
    return pl.pallas_call(
        functools.partial(step_kernel, n_flow, n_grad),
        out_shape=(
            jax.ShapeDtypeStruct(populations.shape, f32),
            jax.ShapeDtypeStruct(sphere_velocity.shape, f32),
            jax.ShapeDtypeStruct(sphere_velocity.shape, f32),
        ),
        in_specs=[smem] * 3 + [vmem] * 9,
        out_specs=(vmem, vmem, vmem),
        scratch_shapes=[
            pltpu.VMEM((19, 64, 128), f32),
            pltpu.VMEM((64, 128), f32),
            pltpu.VMEM((5, 8, 128), f32),
            pltpu.VMEM((5, 8, 128), f32),
            pltpu.VMEM((5, 8, 128), f32),
            pltpu.VMEM((5, 8, 128), f32),
            pltpu.VMEM((5, 8, 128), f32),
            pltpu.VMEM((5, 8, 128), f32),
            pltpu.VMEM((5, span, 128), f32),
            pltpu.VMEM((5, span, 128), f32),
            pltpu.VMEM((8, 128), f32),
            pltpu.VMEM((9, 8, 128), f32),
            pltpu.VMEM((64, 128), f32),
            pltpu.VMEM((128, 128), i32),
            pltpu.VMEM((15, PAD + ROWS, 128), i32),
            pltpu.VMEM((2, ROWS + PAD, 128), f32),
            pltpu.VMEM((2, 8, 128), i32),
            pltpu.VMEM((4, 8, 128), f32),
            pltpu.VMEM((SUM_ROWS, 128), i32),
            pltpu.VMEM((SUM_ROWS, 128), i32),
            pltpu.VMEM((6, SUM_ROWS, 128), f32),
            pltpu.VMEM((9, 8, 128), f32),
            pltpu.VMEM((9, 8, 128), f32),
            dma((2,)),
            dma((2,)),
            dma((n_flow,)),
            dma((n_flow,)),
            dma((n_flow,)),
            dma((n_flow,)),
            dma((9,)),
            dma((9,)),
            dma((9,)),
            dma((9,)),
        ],
        compiler_params=pltpu.CompilerParams(
            collective_id=0, has_side_effects=True, vmem_limit_bytes=40 * 1024 * 1024
        ),
        name="lattice_step",
    )(
        le_offset,
        link_count,
        pair_count,
        populations,
        sphere_velocity,
        link_cell.reshape(128, 128),
        link_dir.reshape(128, 128),
        link_sphere.reshape(128, 128),
        pair_first,
        pair_second,
        pair_gap,
        pair_normal,
    )


def solution(mesh):
    tiled = P(None, "flow", "grad", None)
    listed = P("flow", "grad", None)
    counted = P("flow", "grad")
    return jax.shard_map(
        functools.partial(per_device, mesh.shape["flow"], mesh.shape["grad"]),
        mesh=mesh,
        in_specs=(tiled, P(), tiled, listed, listed, listed, counted, listed, listed, counted, listed, tiled),
        out_specs=(tiled, tiled, tiled),
        check_vma=False,
    )
```

time: 471 us -> 47.8 us (0.10)
  local copies, waits for them, and re-layouts: 285 us -> 6.22 us
  other arithmetic: 118 us -> 0 us
  Pallas kernels: 0 us -> 38.6 us
  starting transfers between devices: 30.1 us -> 0 us
  waiting for transfers between devices: 22.1 us -> 0 us
  matrix products: 5.84 us -> 0 us
    gather x11 -> x0, local copies, waits for them, and re-layouts: 210 us -> none  [the longest x1 90.5 us: tile_links(): bounced = leaving - 6.0 * picked[3] * density[link_cell] * c_dot_u]
    scatter-add x1 -> x0, other arithmetic: 90.4 us -> none  [tile_links(): jax.ops.segment_sum(values.T, sphere_refs, num_segments=9 * slot_count)]
    scatter x3 -> x0, local copies, waits for them, and re-layouts: 62 us -> none  [the longest x1 60.6 us: tile_links(): propagated.reshape(-1).at[target].set(bounced, mode='drop')]
    pallas_call x0 -> x1, Pallas kernels: none -> 38.6 us  [per_device(): pl.pallas_call(functools.partial(step_kernel, n_flow, n_grad), out_shape=...]
    ppermute x16 -> x0, starting transfers between devices: 30.1 us -> none  [the longest x6 16.2 us: padded(): lax.ppermute(lax.slice_in_dim(block, 0, width, axis=dim), axis, backward)]
    ppermute x16 -> x0, waiting for transfers between devices: 22.1 us -> none  [the longest x6 9.85 us: padded(): lax.ppermute(lax.slice_in_dim(block, block.shape[dim] - width, None, axis...]
    unnamed x28 -> x0, other arithmetic: 12.6 us -> none
    reduce_sum x5 -> x0, other arithmetic: 9.72 us -> none  [the longest x1 8.37 us: tile_links(): leaving = jnp.sum(onehot * relaxed[:, link_cell], axis=0)]
  transfers between devices with their start and end apart: 16 -> 0, of which waited for: 10 -> 0; matrix products, arithmetic and copies ran while one was open for 74% -> 0% of each run, Pallas kernels for 0% -> 0%
where the time goes in v1:
time: 47.8 us; the launch traced here: 47.5 us
  Pallas kernels  38.6 us (81%)
  local copies, waits for them, and re-layouts  6.22 us (13%)
  between operations  2.66 us (6%)
    pallas_call x1, Pallas kernels, per_device(): pl.pallas_call(functools.partial(step_kernel, n_flow, n_grad), out_shape=...  38.6 us
    unnamed x21, local copies, waits for them, and re-layouts  6.22 us

profile of v1, /device:TPU:1, one launch (start us, length us, event | category | flops | bytes accessed | tf_op | source)
XLA Modules:
  0.0 47.5 jit_solution(3453005292571221290)
XLA Ops:
  1.9 0.0 copy-start.7
  1.9 0.0 copy-start.8
  2.6 0.0 copy-start.4
  2.6 0.0 copy-start.5
  2.6 0.0 copy-start.6
  2.6 0.0 copy-done.7
  2.6 0.0 copy-done.8
  2.7 0.6 %copy-done.4 = f32[3,1,1,256]{3,2,1,0:T(1,128)S(1)} copy-done((f32[3,1,1,256]{3,2,1,0:T(1,128)S(1)}, f32[3,1,1,256]{3,2,1,0:T(1,128)}, u32[]{:S(2)}) %copy-start.4) | copy-done | bytes 3096
  3.3 0.0 copy-done.5
  3.3 0.0 copy-done.6
  3.3 0.0 copy-start
  3.3 1.1 %copy-done = f32[19,8,8,128]{3,2,1,0:T(8,128)S(1)} copy-done((f32[19,8,8,128]{3,2,1,0:T(8,128)S(1)}, f32[19,8,8,128]{3,2,1,0:T(8,128)}, u32[]{:S(2)}) %copy-start) | copy-done | bytes 622616
  4.4 0.0 copy-start.1
  4.4 0.8 %copy-done.1 = s32[1,1,16384]{2,1,0:T(1,128)S(1)} copy-done((s32[1,1,16384]{2,1,0:T(1,128)S(1)}, s32[1,1,16384]{2,1,0:T(1,128)}, u32[]{:S(2)}) %copy-start.1) | copy-done | bytes 65560
  5.2 0.0 copy-start.2
  5.2 0.8 %copy-done.2 = s32[1,1,16384]{2,1,0:T(1,128)S(1)} copy-done((s32[1,1,16384]{2,1,0:T(1,128)S(1)}, s32[1,1,16384]{2,1,0:T(1,128)}, u32[]{:S(2)}) %copy-start.2) | copy-done | bytes 65560
  6.1 0.0 copy-start.3
  6.1 0.8 %copy-done.3 = s32[1,1,16384]{2,1,0:T(1,128)S(1)} copy-done((s32[1,1,16384]{2,1,0:T(1,128)S(1)}, s32[1,1,16384]{2,1,0:T(1,128)}, u32[]{:S(2)}) %copy-start.3) | copy-done | bytes 65560
  6.9 38.6 %lattice_step.1 = (f32[19,8,8,128]{3,2,1,0:T(8,128)S(1)}, f32[3,1,1,64]{3,2,1,0:T(1,128)S(1)}, f32[3,1,1,64]{3,2,1,0:T(1,128)S(1)}) custom-call(s32[1]{0:T(128)S(6)} %copy.18.offset_ref, s32[1,1]{1,0:T(1,128)S(6)} %copy.19.link_count_ref, s32[1,1]{1,0:T(1,128)S(6)} %copy.20.pair_count_ref, f32[19,8,8,128]{3,2,1,0:T(8,128)S(1)} %copy-done, ...), custom_call_target="tpu_custom_call" | custom-call | tf_op jit(solution)/shard_map/lattice_step/pallas_call | solution.py:604
  45.5 0.8 %copy.21 = f32[19,8,8,128]{3,2,1,0:T(8,128)} copy(f32[19,8,8,128]{3,2,1,0:T(8,128)S(1)} %get-tuple-element.6) | data formatting | bytes 1245184
  46.3 0.6 %copy.22 = f32[3,1,1,64]{3,2,1,0:T(1,128)} copy(f32[3,1,1,64]{3,2,1,0:T(1,128)S(1)} %get-tuple-element.7) | data formatting | bytes 1536
  46.9 0.6 %copy.23 = f32[3,1,1,64]{3,2,1,0:T(1,128)} copy(f32[3,1,1,64]{3,2,1,0:T(1,128)S(1)} %get-tuple-element.8) | data formatting | bytes 1536
Async XLA Ops:
  1.9 0.7 %copy-start.7 = (s32[1,1,256]{2,1,0:T(1,128)S(1)}, s32[1,1,256]{2,1,0:T(1,128)}, u32[]{:S(2)}) copy-start(s32[1,1,256]{2,1,0:T(1,128)} %second_ref.1) | copy-start | bytes 3076
  1.9 0.7 %copy-start.8 = (f32[1,1,256]{2,1,0:T(1,128)S(1)}, f32[1,1,256]{2,1,0:T(1,128)}, u32[]{:S(2)}) copy-start(f32[1,1,256]{2,1,0:T(1,128)} %gap_ref.1) | copy-start | bytes 3076
  2.6 0.7 %copy-start.4 = (f32[3,1,1,256]{3,2,1,0:T(1,128)S(1)}, f32[3,1,1,256]{3,2,1,0:T(1,128)}, u32[]{:S(2)}) copy-start(f32[3,1,1,256]{3,2,1,0:T(1,128)} %normal_ref.1) | copy-start | bytes 9220
  2.6 0.7 %copy-start.5 = (f32[3,1,1,64]{3,2,1,0:T(1,128)S(1)}, f32[3,1,1,64]{3,2,1,0:T(1,128)}, u32[]{:S(2)}) copy-start(f32[3,1,1,64]{3,2,1,0:T(1,128)} %velocity_ref.1) | copy-start | bytes 2308
  2.6 0.7 %copy-start.6 = (s32[1,1,256]{2,1,0:T(1,128)S(1)}, s32[1,1,256]{2,1,0:T(1,128)}, u32[]{:S(2)}) copy-start(s32[1,1,256]{2,1,0:T(1,128)} %first_ref.1) | copy-start | bytes 3076
  3.3 1.1 %copy-start = (f32[19,8,8,128]{3,2,1,0:T(8,128)S(1)}, f32[19,8,8,128]{3,2,1,0:T(8,128)}, u32[]{:S(2)}) copy-start(f32[19,8,8,128]{3,2,1,0:T(8,128)} %pop_ref.1) | copy-start | bytes 1867780
  4.4 0.8 %copy-start.1 = (s32[1,1,16384]{2,1,0:T(1,128)S(1)}, s32[1,1,16384]{2,1,0:T(1,128)}, u32[]{:S(2)}) copy-start(s32[1,1,16384]{2,1,0:T(1,128)} %param.15) | copy-start | bytes 196612
  5.2 0.8 %copy-start.2 = (s32[1,1,16384]{2,1,0:T(1,128)S(1)}, s32[1,1,16384]{2,1,0:T(1,128)}, u32[]{:S(2)}) copy-start(s32[1,1,16384]{2,1,0:T(1,128)} %param.16) | copy-start | bytes 196612
  6.1 0.8 %copy-start.3 = (s32[1,1,16384]{2,1,0:T(1,128)S(1)}, s32[1,1,16384]{2,1,0:T(1,128)}, u32[]{:S(2)}) copy-start(s32[1,1,16384]{2,1,0:T(1,128)} %param.17) | copy-start | bytes 196612

commit v2 on v1

--- a/solution.py
+++ b/solution.py
@@ -41,10 +41,12 @@
 GAP_CUTOFF = 1.0
 INV_MASS = 1.0 / 523.6
 
-LANES = 128
-ROWS = 18 * 64
-PAD = 64
 REF_BITS = 10
+LANE_UNROLL = 16
+ROW_UNROLL = 9
+BACK_LANE_UNROLL = 8
+BACK_ROW_UNROLL = 9
+SUM_UNROLL = 17
 DEAD = 1 << 30
 LINK_ROWS = 128
 SUM_ROWS = LINK_ROWS + 8
@@ -145,6 +147,18 @@
     offset_ref,
     link_count_ref,
     pair_count_ref,
+    pop_hbm,
+    velocity_hbm,
+    cell_hbm,
+    dir_hbm,
+    sphere_hbm,
+    first_hbm,
+    second_hbm,
+    gap_hbm,
+    normal_hbm,
+    next_ref,
+    force_ref,
+    moved_ref,
     pop_ref,
     velocity_ref,
     cell_ref,
@@ -154,9 +168,7 @@
     second_ref,
     gap_ref,
     normal_ref,
-    next_ref,
-    force_ref,
-    moved_ref,
+    in_sem,
     relaxed,
     density,
     face_right,
@@ -171,8 +183,13 @@
     near,
     speed_rows,
     sorted_keys,
+    rests,
+    homes,
     spread,
+    bounced,
     strength,
+    rim,
+    pushes,
     pair_ints,
     pair_floats,
     sum_code,
@@ -200,6 +217,23 @@
     def column(step):
         return lax.rem(flow + n_flow - 1 + step, n_flow)
 
+    copies_in = {}
+
+    def bring(name, source, target):
+        copies_in[name] = pltpu.make_async_copy(source, target, in_sem.at[len(copies_in)])
+        copies_in[name].start()
+
+    bring("velocity", velocity_hbm, velocity_ref)
+    for x in range(8):
+        bring(x, pop_hbm.at[:, x], pop_ref.at[:, x])
+    bring("dir", dir_hbm, dir_ref)
+    bring("cell", cell_hbm, cell_ref)
+    bring("sphere", sphere_hbm, sphere_ref)
+    bring("first", first_hbm, first_ref)
+    bring("second", second_hbm, second_ref)
+    bring("gap", gap_hbm, gap_ref)
+    bring("normal", normal_hbm, normal_ref)
+
     barrier = pltpu.get_barrier_semaphore()
     for target in (left, right):
         pl.semaphore_signal(barrier, inc=1, device_id=(target, grad), device_id_type=MESH)
@@ -215,6 +249,7 @@
     lax.fori_loop(0, up_targets, greet_up, 0)
     lax.fori_loop(0, down_targets, greet_down, 0)
 
+    copies_in["velocity"].wait()
     for axis_id in range(3):
         own_speed[axis_id : axis_id + 1, 0:64] = velocity_ref[axis_id, 0]
 
@@ -226,14 +261,14 @@
         density[rows, :] = total
         return carry
 
+    for x in range(8):
+        copies_in[x].wait()
     lax.fori_loop(0, 8, collide_slab, 0)
     for slot in range(5):
         face_right[slot] = relaxed[RIGHTWARD[slot], 56:64, :]
         face_left[slot] = relaxed[LEFTWARD[slot], 0:8, :]
         face_up[slot] = relaxed[UPWARD[slot], pl.ds(7, 8, stride=8), :]
         face_down[slot] = relaxed[DOWNWARD[slot], pl.ds(0, 8, stride=8), :]
-
-    pl.semaphore_wait(barrier, 2 + up_targets + down_targets)
 
     def speed_copy(code):
         target = (
@@ -313,50 +348,76 @@
         down_copy(column(step), flow).start()
         return carry
 
-    lax.fori_loop(0, up_targets, send_up, 0)
-    lax.fori_loop(0, down_targets, send_down, 0)
-    for copy in face_copies():
-        copy.start()
-    for code in neighbours:
-        speed_copy(code).start()
-
-    number = iota((128, 128), 0) * 128 + iota((128, 128), 1)
-    packed = (((dir_ref[...] - 1) * 8192 + cell_ref[...]) << REF_BITS) + sphere_ref[...]
-    packed = jnp.where(number < link_count_ref[0, 0], packed, DEAD)
+    def send_all():
+        pl.semaphore_wait(barrier, 2 + up_targets + down_targets)
+        for code in neighbours:
+            speed_copy(code).start()
+        for copy in face_copies():
+            copy.start()
+        lax.fori_loop(0, up_targets, send_up, 0)
+        lax.fori_loop(0, down_targets, send_down, 0)
+
+    sends_later = jnp.logical_and(jnp.logical_or(grad == 0, grad == n_grad - 1), flow < n_flow // 2)
+    pl.when(jnp.logical_not(sends_later))(send_all)
+
+    copies_in["dir"].wait()
+    copies_in["cell"].wait()
+    copies_in["sphere"].wait()
+    kinds, cells = dir_ref[...] - 1, cell_ref[...]
+    packed = ((kinds >> 1) << 24) | ((cells & 127) << 17) | ((kinds & 1) << 16) | ((cells >> 7) << REF_BITS) | sphere_ref[...]
+    listed = iota((128, 128), 0) * 128 + iota((128, 128), 1)
+    packed = jnp.where(listed < link_count_ref[0, 0], packed, DEAD)
     ordered = bitonic_sort(packed.reshape(16, 8, 128))
     sorted_keys[...] = ordered.reshape(128, 128)
     picked = [sorted_keys[pl.ds(sublane, 16, stride=8), :] for sublane in range(8)]
-    natural = jnp.transpose(jnp.concatenate(picked, axis=0))
+    natural = jnp.concatenate(picked, axis=0)
     sorted_keys[...] = natural
+    number = iota((128, 128), 1) * 128 + iota((128, 128), 0)
     lag = natural - (number << REF_BITS)
-    rest = lag & ((1 << 24) - 1)
-    home = lag >> 24
-    nothing = jnp.full((PAD, 128), -1, jnp.int32)
-    for level in range(15):
-        spread[level, 0:PAD, :] = nothing
-    for block in range(9):
-        spread[14, PAD + block * 128 : PAD + block * 128 + 128, :] = jnp.where(home == block, rest, -1)
-    lane = iota((128, 128), 1)
-
-    def spread_level(bit):
-        unit = 1 << (bit + REF_BITS)
-
-        def block_of(block, carry):
-            base = pl.multiple_of(block * 128, 128)
-            here = spread[bit + 1, pl.ds(base + PAD, 128), :]
-            if bit >= 7:
-                coming = spread[bit + 1, pl.ds(base + (PAD - (1 << (bit - 7))), 128), :]
-            else:
-                before = spread[bit + 1, pl.ds(base + (PAD - 1), 128), :]
-                coming = pltpu.roll(jnp.where(lane >= 128 - (1 << bit), before, here), 1 << bit, 1)
-            stays = jnp.where(here < unit, here, -1)
-            spread[bit, pl.ds(base + PAD, 128), :] = jnp.where(coming >= unit, coming - unit, stays)
-            return carry
-
-        lax.fori_loop(0, 9, block_of, 0)
-
-    for bit in range(13, -1, -1):
-        spread_level(bit)
+    rests[...] = (lag & ((1 << 24) - 1)).reshape(16, 8, 128)
+    homes[...] = (lag >> 24).reshape(16, 8, 128)
+    for level in range(1, 8):
+        spread[level, 0] = jnp.full((16, 8, 128), -1, jnp.int32)
+
+    def advance(held, coming, unit):
+        return jnp.where(coming >= unit, coming - unit, jnp.where(held < unit, held, -1))
+
+    def spread_lanes(line, carry):
+        rest, home = rests[line], homes[line]
+        lane = iota((9, 8, 128), 2)
+        edge = jnp.full((1, 8, 128), -1, jnp.int32)
+        held = jnp.stack([jnp.where(home == block, rest, -1) for block in range(9)])
+        for bit in range(13, 6, -1):
+            spread[bit + 1, 1:10, line] = held
+            step = 1 << (bit - 7)
+            before = jnp.concatenate([edge, held[:8]], axis=0)
+            coming = pltpu.roll(jnp.where(lane >= 128 - step, before, held), step, 2)
+            held = advance(held, coming, 1 << (bit + REF_BITS))
+        spread[7, 1:10, line] = held
+        return carry
+
+    lax.fori_loop(0, 16, spread_lanes, 0, unroll=LANE_UNROLL)
+
+    def spread_rows(block, carry):
+        sublane = iota((16, 8, 128), 1)
+        held = spread[7, block + 1]
+        for bit in range(6, -1, -1):
+            if bit < 6:
+                spread[bit + 1, block + 1] = held
+            count = max(1 << bit, 8) // 8
+            last = iota((count, 8, 128), 2) == 127
+            around = jnp.where(last, spread[bit + 1, block, 16 - count : 16], held[16 - count :])
+            before = jnp.concatenate([pltpu.roll(around, 1, 2), held[: 16 - count]], axis=0)
+            if bit < 3:
+                step = 1 << bit
+                before = pltpu.roll(jnp.where(sublane >= 8 - step, before, held), step, 1)
+            held = advance(held, before, 1 << (bit + REF_BITS))
+        spread[0, block + 1] = held
+        return carry
+
+    lax.fori_loop(0, 9, spread_rows, 0, unroll=ROW_UNROLL)
+
+    pl.when(sends_later)(send_all)
 
     for code in neighbours:
         speed_copy(code).wait_recv()
@@ -391,6 +452,131 @@
             found = jnp.where(group == pair, take(row, lanes), found)
         return found
 
+    for direction in range(1, 19):
+        sign = 1.0 if direction % 2 == 1 else -1.0
+        pair, part = (direction - 1) // 2, (direction - 1) % 2
+        refs = spread[0, 1 + pair, 8 * part : 8 * part + 8].reshape(64, 128)
+        leaving = relaxed[direction]
+        back = leaving - (6.0 * WEIGHTS[direction] * sign) * density[...] * speed_of(pair, refs)
+        bounced[pair, 8 * part : 8 * part + 8] = back.reshape(8, 8, 128)
+        strength[pair, 8 * part : 8 * part + 8] = (leaving + back).reshape(8, 8, 128)
+
+    def gather_rows(turn, carry):
+        block = 8 - turn
+        sublane = iota((16, 8, 128), 1)
+        held = strength[block]
+        for bit in range(7):
+            count = max(1 << bit, 8) // 8
+            first = iota((count, 8, 128), 2) == 0
+            around = jnp.where(first, rim[bit, 0:count], held[:count])
+            rim[bit, 0:count] = held[:count]
+            after = jnp.concatenate([held[count:], pltpu.roll(around, 127, 2)], axis=0)
+            if bit < 3:
+                step = 1 << bit
+                after = pltpu.roll(jnp.where(sublane < step, after, held), 8 - step, 1)
+            held = jnp.where(spread[bit + 1, block + 1] >= 1 << (bit + REF_BITS), after, held)
+        strength[block] = held
+        return carry
+
+    lax.fori_loop(0, 9, gather_rows, 0, unroll=BACK_ROW_UNROLL)
+
+    def gather_lanes(line, carry):
+        lane = iota((9, 8, 128), 2)
+        held = strength[:, line]
+        for bit in range(7, 14):
+            step = 1 << (bit - 7)
+            after = jnp.concatenate([held[1:], held[8:]], axis=0)
+            ahead = pltpu.roll(jnp.where(lane < step, after, held), 128 - step, 2)
+            held = jnp.where(spread[bit + 1, 1:10, line] >= 1 << (bit + REF_BITS), ahead, held)
+        home = homes[line]
+        push = jnp.zeros((8, 128), jnp.float32)
+        for block in range(9):
+            push = jnp.where(home == block, held[block], push)
+        pushes[line] = push
+        return carry
+
+    lax.fori_loop(0, 16, gather_lanes, 0, unroll=BACK_LANE_UNROLL)
+    keys = sorted_keys[...]
+    push = pushes[...].reshape(128, 128)
+
+    def put_terms(rows, refs, terms):
+        sum_code[rows, :] = refs >> 6
+        sum_slot[rows, :] = refs & 63
+        for axis_id in range(3):
+            coarse = terms[axis_id].astype(jnp.bfloat16).astype(jnp.float32)
+            sum_piece[axis_id, rows, :] = coarse
+            sum_piece[3 + axis_id, rows, :] = terms[axis_id] - coarse
+
+    kind = (((keys >> 24) << 1) | ((keys >> 16) & 1)) & 127
+    small_lane = iota((8, 128), 1)
+    terms = []
+    for axis_id in range(3):
+        table = jnp.zeros((8, 128), jnp.float32)
+        for direction in range(1, 19):
+            part = VELOCITIES[direction][axis_id]
+            if part != 0:
+                table = jnp.where(small_lane == direction - 1, float(part), table)
+        tall_table = jnp.concatenate([table] * 16, axis=0)
+        terms.append(take(tall_table, kind) * push)
+    put_terms(pl.ds(0, 128), keys & 1023, terms)
+
+    for name in ("first", "second", "gap", "normal"):
+        copies_in[name].wait()
+    pair_ints[...] = jnp.zeros((2, 8, 128), jnp.int32)
+    pair_floats[...] = jnp.ones((4, 8, 128), jnp.float32)
+    for row in range(2):
+        lanes = slice(row * 128, row * 128 + 128)
+        pair_ints[0, row : row + 1, :] = first_ref[0, :, lanes] + 256
+        pair_ints[1, row : row + 1, :] = second_ref[0, :, lanes]
+        pair_floats[3, row : row + 1, :] = gap_ref[0, :, lanes]
+        for axis_id in range(3):
+            pair_floats[axis_id, row : row + 1, :] = normal_ref[axis_id, 0, :, lanes]
+    heads, tails = pair_ints[0], pair_ints[1]
+    normals = [pair_floats[axis_id] for axis_id in range(3)]
+    rate = None
+    for axis_id in range(3):
+        gap_speed = (speed_of(9 + axis_id, heads) - speed_of(9 + axis_id, tails)) * normals[axis_id]
+        rate = gap_speed if rate is None else rate + gap_speed
+    resist = LUB_COEF * (1.0 / jnp.maximum(pair_floats[3], GAP_FLOOR) - 1.0 / GAP_CUTOFF)
+    alive = iota((8, 128), 0) * 128 + small_lane < jnp.minimum(pair_count_ref[0, 0], 256)
+    scale = jnp.where(alive, -resist * rate, 0.0)
+    lift = [scale * normals[axis_id] for axis_id in range(3)]
+    lower = iota((8, 128), 0) < 2
+    both = jnp.where(lower, heads, pltpu.roll(tails, 2, 0))
+    lift = [jnp.where(lower, term, -pltpu.roll(term, 2, 0)) for term in lift]
+    put_terms(pl.ds(128, 8), both, lift)
+
+    code_rows = iota((16, 128), 0)
+    slot_rows = iota((64, 128), 0)
+
+    def add_rows(group, total):
+        base = group * 8
+        pieces, slots = [], []
+        for row in range(8):
+            at = pl.ds(base + row, 1)
+            chosen = code_rows == jnp.broadcast_to(sum_code[at, :], (16, 128))
+            parts = [
+                jnp.where(chosen, jnp.broadcast_to(sum_piece[piece, at, :], (16, 128)), 0.0).astype(jnp.bfloat16)
+                for piece in range(6)
+            ]
+            pieces.append(jnp.concatenate(parts, axis=0))
+            slot = slot_rows == jnp.broadcast_to(sum_slot[at, :], (64, 128))
+            slots.append(jnp.where(slot, 1.0, 0.0).astype(jnp.bfloat16))
+        return total + lax.dot_general(
+            jnp.concatenate(pieces, axis=1),
+            jnp.concatenate(slots, axis=1),
+            (((1,), (1,)), ((), ())),
+            preferred_element_type=jnp.float32,
+        )
+
+    total = lax.fori_loop(0, SUM_ROWS // 8, add_rows, jnp.zeros((96, 64), jnp.float32), unroll=SUM_UNROLL)
+    for axis_id in range(3):
+        summed = total[16 * axis_id : 16 * axis_id + 16] + total[48 + 16 * axis_id : 64 + 16 * axis_id]
+        for code in range(9):
+            part_out[code, axis_id : axis_id + 1, 0:64] = summed[code : code + 1]
+
+    for code in neighbours:
+        part_copy(code).start()
     def came_up(step, carry):
         up_copy(column(step), column(step)).wait_recv()
         return carry
@@ -441,118 +627,11 @@
     next_ref[0] = relaxed[0].reshape(8, 8, 128)
     for direction in range(1, 19):
         opposite = direction + 1 if direction % 2 == 1 else direction - 1
-        sign = 1.0 if direction % 2 == 1 else -1.0
-        refs = spread[0, PAD + 64 * (direction - 1) : PAD + 64 * direction, :]
-        leaving = relaxed[direction]
-        wall = speed_of((direction - 1) // 2, refs)
-        bounced = leaving - (6.0 * WEIGHTS[direction] * sign) * density[...] * wall
-        strength[0, 64 * (direction - 1) : 64 * direction, :] = leaving + bounced
-        updated = jnp.where(refs >= 0, bounced, propagated(opposite))
-        next_ref[opposite] = updated.reshape(8, 8, 128)
-
-    def gather_level(bit):
-        unit = 1 << (bit + REF_BITS)
-        now, later = bit % 2, (bit + 1) % 2
-
-        def block_of(block, carry):
-            base = pl.multiple_of(block * 128, 128)
-            moves = spread[bit + 1, pl.ds(base + PAD, 128), :] >= unit
-            here = strength[now, pl.ds(base, 128), :]
-            if bit >= 7:
-                ahead = strength[now, pl.ds(base + (1 << (bit - 7)), 128), :]
-            else:
-                after = strength[now, pl.ds(base + 1, 128), :]
-                ahead = pltpu.roll(jnp.where(lane < (1 << bit), after, here), 128 - (1 << bit), 1)
-            strength[later, pl.ds(base, 128), :] = jnp.where(moves, ahead, here)
-            return carry
-
-        lax.fori_loop(0, 9, block_of, 0)
-
-    for bit in range(14):
-        gather_level(bit)
-    keys = sorted_keys[...]
-    lag = keys - (number << REF_BITS)
-    home = lag >> 24
-    push = jnp.zeros((128, 128), jnp.float32)
-    for block in range(9):
-        push = jnp.where(home == block, strength[0, block * 128 : block * 128 + 128, :], push)
-
-    def put_terms(rows, refs, terms):
-        sum_code[rows, :] = refs >> 6
-        sum_slot[rows, :] = refs & 63
-        for axis_id in range(3):
-            coarse = terms[axis_id].astype(jnp.bfloat16).astype(jnp.float32)
-            sum_piece[axis_id, rows, :] = coarse
-            sum_piece[3 + axis_id, rows, :] = terms[axis_id] - coarse
-
-    kind = (keys >> 23) & 127
-    small_lane = iota((8, 128), 1)
-    terms = []
-    for axis_id in range(3):
-        table = jnp.zeros((8, 128), jnp.float32)
-        for direction in range(1, 19):
-            part = VELOCITIES[direction][axis_id]
-            if part != 0:
-                table = jnp.where(small_lane == direction - 1, float(part), table)
-        tall_table = jnp.concatenate([table] * 16, axis=0)
-        terms.append(take(tall_table, kind) * push)
-    put_terms(pl.ds(0, 128), keys & 1023, terms)
-
-    pair_ints[...] = jnp.zeros((2, 8, 128), jnp.int32)
-    pair_floats[...] = jnp.ones((4, 8, 128), jnp.float32)
-    for row in range(2):
-        lanes = slice(row * 128, row * 128 + 128)
-        pair_ints[0, row : row + 1, :] = first_ref[0, :, lanes] + 256
-        pair_ints[1, row : row + 1, :] = second_ref[0, :, lanes]
-        pair_floats[3, row : row + 1, :] = gap_ref[0, :, lanes]
-        for axis_id in range(3):
-            pair_floats[axis_id, row : row + 1, :] = normal_ref[axis_id, 0, :, lanes]
-    heads, tails = pair_ints[0], pair_ints[1]
-    normals = [pair_floats[axis_id] for axis_id in range(3)]
-    rate = None
-    for axis_id in range(3):
-        gap_speed = (speed_of(9 + axis_id, heads) - speed_of(9 + axis_id, tails)) * normals[axis_id]
-        rate = gap_speed if rate is None else rate + gap_speed
-    resist = LUB_COEF * (1.0 / jnp.maximum(pair_floats[3], GAP_FLOOR) - 1.0 / GAP_CUTOFF)
-    alive = iota((8, 128), 0) * 128 + small_lane < jnp.minimum(pair_count_ref[0, 0], 256)
-    scale = jnp.where(alive, -resist * rate, 0.0)
-    lift = [scale * normals[axis_id] for axis_id in range(3)]
-    lower = iota((8, 128), 0) < 2
-    both = jnp.where(lower, heads, pltpu.roll(tails, 2, 0))
-    lift = [jnp.where(lower, term, -pltpu.roll(term, 2, 0)) for term in lift]
-    put_terms(pl.ds(128, 8), both, lift)
-
-    code_rows = iota((16, 128), 0)
-    slot_rows = iota((64, 128), 0)
-
-    def add_rows(group, total):
-        base = group * 8
-        pieces, slots = [], []
-        for row in range(8):
-            at = pl.ds(base + row, 1)
-            chosen = code_rows == jnp.broadcast_to(sum_code[at, :], (16, 128))
-            parts = [
-                jnp.where(chosen, jnp.broadcast_to(sum_piece[piece, at, :], (16, 128)), 0.0).astype(jnp.bfloat16)
-                for piece in range(6)
-            ]
-            pieces.append(jnp.concatenate(parts, axis=0))
-            slot = slot_rows == jnp.broadcast_to(sum_slot[at, :], (64, 128))
-            slots.append(jnp.where(slot, 1.0, 0.0).astype(jnp.bfloat16))
-        return total + lax.dot_general(
-            jnp.concatenate(pieces, axis=1),
-            jnp.concatenate(slots, axis=1),
-            (((1,), (1,)), ((), ())),
-            preferred_element_type=jnp.float32,
-        )
-
-    total = lax.fori_loop(0, SUM_ROWS // 8, add_rows, jnp.zeros((96, 64), jnp.float32))
-    for axis_id in range(3):
-        summed = total[16 * axis_id : 16 * axis_id + 16] + total[48 + 16 * axis_id : 64 + 16 * axis_id]
-        for code in range(9):
-            part_out[code, axis_id : axis_id + 1, 0:64] = summed[code : code + 1]
-
-    for code in neighbours:
-        part_copy(code).start()
+        pair, part = (direction - 1) // 2, (direction - 1) % 2
+        refs = spread[0, 1 + pair, 8 * part : 8 * part + 8]
+        back = bounced[pair, 8 * part : 8 * part + 8]
+        next_ref[opposite] = jnp.where(refs >= 0, back, propagated(opposite).reshape(8, 8, 128))
+
     forces = part_out[4]
     for code in neighbours:
         part_copy(code).wait_recv()
@@ -578,6 +657,19 @@
 
     lax.fori_loop(0, up_targets, sent_up, 0)
     lax.fori_loop(0, down_targets, sent_down, 0)
+
+
+def hand_over(next_in, force_in, moved_in, next_out, force_out, moved_out, sem):
+    copies = [
+        pltpu.make_async_copy(force_in, force_out, sem.at[0]),
+        pltpu.make_async_copy(moved_in, moved_out, sem.at[1]),
+    ]
+    for part, (start, end) in enumerate(((0, 5), (5, 10), (10, 15), (15, 19))):
+        copies.append(pltpu.make_async_copy(next_in.at[start:end], next_out.at[start:end], sem.at[2 + part]))
+    for copy in copies:
+        copy.start()
+    for copy in copies:
+        copy.wait()
 
 
 def per_device(
@@ -597,20 +689,31 @@
     pair_normal,
 ):
     vmem = pl.BlockSpec(memory_space=pltpu.VMEM)
+    hbm = pl.BlockSpec(memory_space=pltpu.HBM)
     smem = pl.BlockSpec(memory_space=pltpu.SMEM)
     span = 8 * n_flow
     f32, i32 = jnp.float32, jnp.int32
     dma = pltpu.SemaphoreType.DMA
-    return pl.pallas_call(
+    results = pl.pallas_call(
         functools.partial(step_kernel, n_flow, n_grad),
         out_shape=(
-            jax.ShapeDtypeStruct(populations.shape, f32),
-            jax.ShapeDtypeStruct(sphere_velocity.shape, f32),
-            jax.ShapeDtypeStruct(sphere_velocity.shape, f32),
+            pltpu.VMEM(populations.shape, f32),
+            pltpu.VMEM(sphere_velocity.shape, f32),
+            pltpu.VMEM(sphere_velocity.shape, f32),
         ),
-        in_specs=[smem] * 3 + [vmem] * 9,
+        in_specs=[smem] * 3 + [hbm] * 9,
         out_specs=(vmem, vmem, vmem),
         scratch_shapes=[
+            pltpu.VMEM((19, 8, 8, 128), f32),
+            pltpu.VMEM((3, 1, 1, 64), f32),
+            pltpu.VMEM((128, 128), i32),
+            pltpu.VMEM((128, 128), i32),
+            pltpu.VMEM((128, 128), i32),
+            pltpu.VMEM((1, 1, 256), i32),
+            pltpu.VMEM((1, 1, 256), i32),
+            pltpu.VMEM((1, 1, 256), f32),
+            pltpu.VMEM((3, 1, 1, 256), f32),
+            dma((16,)),
             pltpu.VMEM((19, 64, 128), f32),
             pltpu.VMEM((64, 128), f32),
             pltpu.VMEM((5, 8, 128), f32),
@@ -625,8 +728,13 @@
             pltpu.VMEM((9, 8, 128), f32),
             pltpu.VMEM((64, 128), f32),
             pltpu.VMEM((128, 128), i32),
-            pltpu.VMEM((15, PAD + ROWS, 128), i32),
-            pltpu.VMEM((2, ROWS + PAD, 128), f32),
+            pltpu.VMEM((16, 8, 128), i32),
+            pltpu.VMEM((16, 8, 128), i32),
+            pltpu.VMEM((15, 10, 16, 8, 128), i32),
+            pltpu.VMEM((9, 16, 8, 128), f32),
+            pltpu.VMEM((9, 16, 8, 128), f32),
+            pltpu.VMEM((7, 8, 8, 128), f32),
+            pltpu.VMEM((16, 8, 128), f32),
             pltpu.VMEM((2, 8, 128), i32),
             pltpu.VMEM((4, 8, 128), f32),
             pltpu.VMEM((SUM_ROWS, 128), i32),
@@ -653,16 +761,30 @@
         le_offset,
         link_count,
         pair_count,
-        populations,
-        sphere_velocity,
-        link_cell.reshape(128, 128),
-        link_dir.reshape(128, 128),
-        link_sphere.reshape(128, 128),
-        pair_first,
-        pair_second,
-        pair_gap,
-        pair_normal,
+        *[
+            pltpu.with_memory_space_constraint(operand, pltpu.HBM)
+            for operand in (
+                populations,
+                sphere_velocity,
+                link_cell.reshape(128, 128),
+                link_dir.reshape(128, 128),
+                link_sphere.reshape(128, 128),
+                pair_first,
+                pair_second,
+                pair_gap,
+                pair_normal,
+            )
+        ],
     )
+    return pl.pallas_call(
+        hand_over,
+        out_shape=[jax.ShapeDtypeStruct(result.shape, f32) for result in results],
+        in_specs=[vmem] * 3,
+        out_specs=[hbm] * 3,
+        scratch_shapes=[dma((6,))],
+        compiler_params=pltpu.CompilerParams(vmem_limit_bytes=40 * 1024 * 1024),
+        name="hand_over",
+    )(*results)
 
 
 def solution(mesh):

time: 47.8 us -> 32.1 us (0.67)
  Pallas kernels: 38.6 us -> 29.4 us
  local copies, waits for them, and re-layouts: 6.22 us -> 0 us
    pallas_call x1, Pallas kernels: 38.6 us -> 28.5 us  [per_device(): pl.pallas_call(functools.partial(step_kernel, n_flow, n_grad), out_shape=...]
    unnamed x21 -> x0, local copies, waits for them, and re-layouts: 6.22 us -> none
    pallas_call x0 -> x1, Pallas kernels: none -> 0.88 us  [per_device(): pl.pallas_call(hand_over, out_shape=[jax.ShapeDtypeStruct(result.shape, f...]
where the time goes in v2:
time: 32.1 us; the launch traced here: 31.9 us
  Pallas kernels  29.4 us (92%)
  between operations  2.58 us (8%)
    pallas_call x1, Pallas kernels, per_device(): pl.pallas_call(functools.partial(step_kernel, n_flow, n_grad), out_shape=...  28.5 us
    pallas_call x1, Pallas kernels, per_device(): pl.pallas_call(hand_over, out_shape=[jax.ShapeDtypeStruct(result.shape, f...  0.88 us

profile of v2, /device:TPU:1, one launch (start us, length us, event | category | flops | bytes accessed | tf_op | source)
XLA Modules:
  0.0 31.9 jit_solution(11151759612046682724)
XLA Ops:
  2.6 28.5 %lattice_step.1 = (f32[19,8,8,128]{3,2,1,0:T(8,128)S(1)}, f32[3,1,1,64]{3,2,1,0:T(1,128)S(1)}, f32[3,1,1,64]{3,2,1,0:T(1,128)S(1)}) custom-call(s32[1]{0:T(128)S(6)} %copy.15.offset_ref, s32[1,1]{1,0:T(1,128)S(6)} %copy.16.link_count_ref, s32[1,1]{1,0:T(1,128)S(6)} %copy.17.pair_count_ref, f32[19,8,8,128]{3,2,1,0:T(8,128)} %pop_hbm.1, ...), custom_call_target="tpu_custom_call" | custom-call | tf_op jit(solution)/shard_map/lattice_step/pallas_call | solution.py:697
  31.1 0.9 %hand_over.1 = (f32[19,8,8,128]{3,2,1,0:T(8,128)}, f32[3,1,1,64]{3,2,1,0:T(1,128)}, f32[3,1,1,64]{3,2,1,0:T(1,128)}) custom-call(f32[19,8,8,128]{3,2,1,0:T(8,128)S(1)} %get-tuple-element.6.next_in, f32[3,1,1,64]{3,2,1,0:T(1,128)S(1)} %get-tuple-element.7.force_in, f32[3,1,1,64]{3,2,1,0:T(1,128)S(1)} %get-tuple-element.8.moved_in), custom_call_target="tpu_custom_call" | custom-call | tf_op jit(solution)/shard_map/hand_over/pallas_call | solution.py:779

commit v3 on v2

--- a/solution.py
+++ b/solution.py
@@ -106,9 +106,18 @@
     return relaxed, density
 
 
-def bitonic_sort(keys):
+def bitonic_sort(keys, rows):
+    def swap(held, slot):
+        rows[slot] = held.reshape(128, 128)
+        parts = [rows[slot, pl.ds(64 * half + line, 8, stride=8), :] for half in range(2) for line in range(8)]
+        return jnp.stack(parts)
+
+    def exchange(held, bit):
+        pairs = held.reshape(8 >> bit, 2, 1 << bit, 8, 128)
+        first, second = pairs[:, 0], pairs[:, 1]
+        return jnp.stack([jnp.minimum(first, second), jnp.maximum(first, second)], axis=1).reshape(16, 8, 128)
+
     place = iota((16, 8, 128), 0) + 16 * iota((16, 8, 128), 1) + 128 * iota((16, 8, 128), 2)
-    sublane = iota((16, 8, 128), 1)
     lane = iota((128, 128), 1)
     for phase in range(1, 15):
         flips = place >> (phase - 1)
@@ -117,27 +126,24 @@
         elif phase < 14:
             flips = flips ^ (place >> phase)
         keys = keys ^ (-(flips & 1))
-        for bit in range(phase - 1, -1, -1):
-            if bit < 4:
-                step = 1 << bit
-                pairs = keys.reshape(8 >> bit, 2, step, 8, 128)
-                first, second = pairs[:, 0], pairs[:, 1]
-                low, high = jnp.minimum(first, second), jnp.maximum(first, second)
-                keys = jnp.stack([low, high], axis=1).reshape(16, 8, 128)
-            elif bit < 7:
-                step = 1 << (bit - 4)
-                upper = (sublane & step) != 0
-                partner = pltpu.roll(keys, step, 1)
-                if step != 4:
-                    partner = jnp.where(upper, partner, pltpu.roll(keys, 8 - step, 1))
-                keys = jnp.where(upper, jnp.maximum(keys, partner), jnp.minimum(keys, partner))
-            else:
-                step = 1 << (bit - 7)
-                flat = keys.reshape(128, 128)
-                partner = take(flat, lane ^ step)
-                upper = (lane & step) != 0
-                flat = jnp.where(upper, jnp.maximum(flat, partner), jnp.minimum(flat, partner))
-                keys = flat.reshape(16, 8, 128)
+        bit = phase - 1
+        while bit >= 7:
+            step = 1 << (bit - 7)
+            flat = keys.reshape(128, 128)
+            partner = take(flat, lane ^ step)
+            upper = (lane & step) != 0
+            flat = jnp.where(upper, jnp.maximum(flat, partner), jnp.minimum(flat, partner))
+            keys = flat.reshape(16, 8, 128)
+            bit -= 1
+        if bit >= 4:
+            keys = swap(keys, phase % 2)
+            while bit >= 4:
+                keys = exchange(keys, bit - 4)
+                bit -= 1
+            keys = swap(keys, phase % 2)
+        while bit >= 0:
+            keys = exchange(keys, bit)
+            bit -= 1
     return keys
 
 
@@ -183,6 +189,7 @@
     near,
     speed_rows,
     sorted_keys,
+    sort_rows,
     rests,
     homes,
     spread,
@@ -298,7 +305,7 @@
             device_id_type=MESH,
         )
 
-    neighbours = [code for code in range(9) if code != 4]
+    neighbours = [0, 2, 6, 8, 1, 7, 3, 5]
 
     def face_copies():
         return (
@@ -367,7 +374,7 @@
     packed = ((kinds >> 1) << 24) | ((cells & 127) << 17) | ((kinds & 1) << 16) | ((cells >> 7) << REF_BITS) | sphere_ref[...]
     listed = iota((128, 128), 0) * 128 + iota((128, 128), 1)
     packed = jnp.where(listed < link_count_ref[0, 0], packed, DEAD)
-    ordered = bitonic_sort(packed.reshape(16, 8, 128))
+    ordered = bitonic_sort(packed.reshape(16, 8, 128), sort_rows)
     sorted_keys[...] = ordered.reshape(128, 128)
     picked = [sorted_keys[pl.ds(sublane, 16, stride=8), :] for sublane in range(8)]
     natural = jnp.concatenate(picked, axis=0)
@@ -632,6 +639,22 @@
         back = bounced[pair, 8 * part : 8 * part + 8]
         next_ref[opposite] = jnp.where(refs >= 0, back, propagated(opposite).reshape(8, 8, 128))
 
+    for code in neighbours:
+        speed_copy(code).wait_send()
+    for copy in face_copies():
+        copy.wait_send()
+
+    def sent_up(step, carry):
+        up_copy(column(step), flow).wait_send()
+        return carry
+
+    def sent_down(step, carry):
+        down_copy(column(step), flow).wait_send()
+        return carry
+
+    lax.fori_loop(0, up_targets, sent_up, 0)
+    lax.fori_loop(0, down_targets, sent_down, 0)
+
     forces = part_out[4]
     for code in neighbours:
         part_copy(code).wait_recv()
@@ -643,20 +666,6 @@
 
     for code in neighbours:
         part_copy(code).wait_send()
-        speed_copy(code).wait_send()
-    for copy in face_copies():
-        copy.wait_send()
-
-    def sent_up(step, carry):
-        up_copy(column(step), flow).wait_send()
-        return carry
-
-    def sent_down(step, carry):
-        down_copy(column(step), flow).wait_send()
-        return carry
-
-    lax.fori_loop(0, up_targets, sent_up, 0)
-    lax.fori_loop(0, down_targets, sent_down, 0)
 
 
 def hand_over(next_in, force_in, moved_in, next_out, force_out, moved_out, sem):
@@ -728,6 +737,7 @@
             pltpu.VMEM((9, 8, 128), f32),
             pltpu.VMEM((64, 128), f32),
             pltpu.VMEM((128, 128), i32),
+            pltpu.VMEM((2, 128, 128), i32),
             pltpu.VMEM((16, 8, 128), i32),
             pltpu.VMEM((16, 8, 128), i32),
             pltpu.VMEM((15, 10, 16, 8, 128), i32),

time: 32.1 us -> 31.8 us (level)
  Pallas kernels: 29.4 us -> 29 us
    pallas_call x1, Pallas kernels: 28.5 us -> 28.1 us  [per_device(): pl.pallas_call(functools.partial(step_kernel, n_flow, n_grad), out_shape=...]
where the time goes in v3:
time: 31.8 us; the launch traced here: 31.6 us
  Pallas kernels  29 us (91%)
  between operations  2.58 us (8%)
    pallas_call x1, Pallas kernels, per_device(): pl.pallas_call(functools.partial(step_kernel, n_flow, n_grad), out_shape=...  28.1 us
    pallas_call x1, Pallas kernels, per_device(): pl.pallas_call(hand_over, out_shape=[jax.ShapeDtypeStruct(result.shape, f...  0.88 us

profile of v3, /device:TPU:1, one launch (start us, length us, event | category | flops | bytes accessed | tf_op | source)
XLA Modules:
  0.0 31.6 jit_solution(2761107510417902436)
XLA Ops:
  2.6 28.1 %lattice_step.1 = (f32[19,8,8,128]{3,2,1,0:T(8,128)S(1)}, f32[3,1,1,64]{3,2,1,0:T(1,128)S(1)}, f32[3,1,1,64]{3,2,1,0:T(1,128)S(1)}) custom-call(s32[1]{0:T(128)S(6)} %copy.15.offset_ref, s32[1,1]{1,0:T(1,128)S(6)} %copy.16.link_count_ref, s32[1,1]{1,0:T(1,128)S(6)} %copy.17.pair_count_ref, f32[19,8,8,128]{3,2,1,0:T(8,128)} %pop_hbm.1, ...), custom_call_target="tpu_custom_call" | custom-call | tf_op jit(solution)/shard_map/lattice_step/pallas_call | solution.py:706
  30.7 0.9 %hand_over.1 = (f32[19,8,8,128]{3,2,1,0:T(8,128)}, f32[3,1,1,64]{3,2,1,0:T(1,128)}, f32[3,1,1,64]{3,2,1,0:T(1,128)}) custom-call(f32[19,8,8,128]{3,2,1,0:T(8,128)S(1)} %get-tuple-element.6.next_in, f32[3,1,1,64]{3,2,1,0:T(1,128)S(1)} %get-tuple-element.7.force_in, f32[3,1,1,64]{3,2,1,0:T(1,128)S(1)} %get-tuple-element.8.moved_in), custom_call_target="tpu_custom_call" | custom-call | tf_op jit(solution)/shard_map/hand_over/pallas_call | solution.py:789
